TPU v7x, 128 devices: a whole 4x4x4 slice. The times are simulated.
128 devices in a mesh: frames: 4 (over z_lo, core), feat: 32 (over z_hi, y, x).
Axes of the slice: x: 4, y: 4, z: 4 (z_hi: 2, z_lo: 2; z = z_hi * 2 + z_lo), core: 2. Of those that a mesh axis runs over, the one named last changes fastest.
Arguments:
- trajectory: bfloat16 [1024, 212992], P(('frames', 'feat'))
- tile_list: int32 [12288, 2], P(('frames', 'feat')), may hold values from 0 to 1663, as said below
Outputs:
- cov_instant: float32 [12288, 128, 128], P(('frames', 'feat'))
- cov_lagged: float32 [12288, 128, 128], P(('frames', 'feat'))
Inputs may be any that keep to these rules, and one draw needn't show every extreme that they name: `tile_list`: the tiles of device d (entries d * 96 to (d + 1) * 96 - 1) have row blocks I from d * 13 - 2 to (d + 1) * 13 + 1 and column blocks J with |I - J| <= 4, all within 0 to 1663; tiles may repeat.
All inputs are finite; a program needn't handle non-finite values.
Results may differ from a plain program's by a relative error of at most 0.004.
Values may be sent and summed in bfloat16 or wider, within the bound.
No kernel may reach another device: no remote copies, remote signals or barrier semaphores. Data moves between devices by JAX's collectives and lax.ppermute only.
A program may use at most 128 MiB of HBM per device.

v0:
```python
import jax
import jax.numpy as jnp
from jax import lax
from jax.sharding import PartitionSpec as P

BS = 128
LAG = 16
BAND = 4
REACH = 2


def extended(cells, sides, width):
    for axis, dim in sides:
        count = lax.axis_size(axis)
        ends = count - 1
        head = lax.slice_in_dim(cells, 0, width, axis=dim)
        tail = lax.slice_in_dim(cells, cells.shape[dim] - width, cells.shape[dim], axis=dim)
        cells = jnp.concatenate(
            [
                lax.ppermute(tail, axis, [(i, (i + 1) % count) for i in range(ends)]),
                cells,
                lax.ppermute(head, axis, [((i + 1) % count, i) for i in range(ends)]),
            ],
            axis=dim,
        )
    return cells


def per_device(trajectory, tile_list):
    panels = lax.all_to_all(trajectory, ("frames", "feat"), split_axis=1, concat_axis=0, tiled=True)
    frame_total = panels.shape[0]
    blocks_here = panels.shape[1] // BS
    column_means = jnp.sum(panels, axis=0, dtype=jnp.float32) / frame_total
    centred = (panels - column_means).astype(jnp.bfloat16)
    margin = REACH + BAND
    window = extended(centred, ((("frames", "feat"), 1),), margin * BS)
    stacked = window.reshape(frame_total, blocks_here + 2 * margin, BS).transpose(1, 0, 2)
    row_span = blocks_here + 2 * REACH
    row_first = margin - REACH
    row_panels = stacked[row_first : row_first + row_span]
    instant_parts = []
    lagged_parts = []
    for offset in range(-BAND, BAND + 1):
        col_panels = stacked[row_first + offset : row_first + offset + row_span]
        instant_parts.append(
            jnp.einsum("rti,rtj->rij", row_panels, col_panels, preferred_element_type=jnp.float32)
        )
        lagged_parts.append(
            jnp.einsum(
                "rti,rtj->rij",
                row_panels[:, : frame_total - LAG],
                col_panels[:, LAG:],
                preferred_element_type=jnp.float32,
            )
        )
    instant_all = jnp.stack(instant_parts, axis=0).reshape((2 * BAND + 1) * row_span, BS, BS)
    lagged_all = jnp.stack(lagged_parts, axis=0).reshape((2 * BAND + 1) * row_span, BS, BS)
    first_row = lax.axis_index(("frames", "feat")) * blocks_here - REACH
    row_local = tile_list[:, 0] - first_row
    offset_local = tile_list[:, 1] - tile_list[:, 0] + BAND
    position = offset_local * row_span + row_local
    instant = jnp.take(instant_all, position, axis=0) / (frame_total - 1)
    lagged = jnp.take(lagged_all, position, axis=0) / (frame_total - LAG)
    return (instant, lagged)


def solution(mesh):
    in_specs = (P(("frames", "feat"), None), P(("frames", "feat"), None))
    out_specs = (P(("frames", "feat"), None, None), P(("frames", "feat"), None, None))
    return jax.shard_map(
        per_device, mesh=mesh, in_specs=in_specs, out_specs=out_specs, check_vma=False
    )
```

profile of v0, /device:TPU:1, one launch (start us, length us, event | category | flops | bytes accessed | tf_op | source)
XLA Modules:
  0.0 189.7 jit_solution(16024420593361691053)
XLA Ops:
  0.6 55.3 %all_to_all.13 = bf16[8,128,1664]{2,0,1:T(8,128)(2,1)S(1)} all-to-all(bf16[8,128,1664]{2,0,1:T(8,128)(2,1)} %bitcast.120), channel_id=1, replica_groups=mesh['frames'=4,'feat'=32] {'frames','feat'}, dimensions={1} | all-to-all | bytes 6815744 | tf_op jit(solution)/shard_map/all_to_all | solution.py:30
  55.9 0.5 convert_reduce_fusion
  56.4 0.0 copy-start.3
  56.4 0.7 fusion.1
  57.1 1.9 fusion.155
  59.0 1.9 %collective-permute-start = (bf16[1024,768]{1,0:T(8,128)(2,1)}, bf16[1024,768]{1,0:T(8,128)(2,1)}, u32[]{:S(2)}, u32[]{:S(2)}) collective-permute-start(bf16[1024,768]{1,0:T(8,128)(2,1)} %get-tuple-element.5), channel_id=1, source_target_pairs={{0,1},{1,2},{2,3},{3,4},{4,5},{5,6},{6,7},{7,8},{8,9},{9,10},{10,1... | collective-permute-start | bytes 4718600 | tf_op jit(solution)/shard_map/ppermute | solution.py:20
  60.9 9.4 %collective-permute-start.1 = (bf16[1024,768]{1,0:T(8,128)(2,1)}, bf16[1024,768]{1,0:T(8,128)(2,1)}, u32[]{:S(2)}, u32[]{:S(2)}) collective-permute-start(bf16[1024,768]{1,0:T(8,128)(2,1)} %get-tuple-element.6), channel_id=1, source_target_pairs={{1,0},{2,1},{3,2},{4,3},{5,4},{6,5},{7,6},{8,7},{9,8},{10,9},{11,1... | collective-permute-start | bytes 4718600 | tf_op jit(solution)/shard_map/ppermute | solution.py:22
  70.3 0.0 copy-done.3
  70.3 0.6 compare_and_fusion
  70.9 0.6 pad_clamp_fusion
  71.5 32.9 %collective-permute-done = bf16[1024,768]{1,0:T(8,128)(2,1)} collective-permute-done((bf16[1024,768]{1,0:T(8,128)(2,1)}, bf16[1024,768]{1,0:T(8,128)(2,1)}, u32[]{:S(2)}, u32[]{:S(2)}) %collective-permute-start) | collective-permute-done | bytes 1572896 | tf_op jit(solution)/shard_map/ppermute | solution.py:20
  104.4 0.0 collective-permute-done.1
  104.4 4.9 %pad_maximum_fusion = bf16[1024,3200]{1,0:T(8,128)(2,1)} fusion(bf16[1024,768]{1,0:T(8,128)(2,1)} %collective-permute-done.1, bf16[1024,1664]{1,0:T(8,128)(2,1)S(1)} %fusion.1, bf16[1024,768]{1,0:T(8,128)(2,1)} %collective-permute-done), kind=kLoop, calls=%fused_computation.6 | loop fusion | flops 19660800 | bytes 13107200 | tf_op jit(solution)/shard_map/concatenate | solution.py:18
  109.3 9.6 %copy.24 = bf16[1024,3200]{0,1:T(8,128)(2,1)} copy(bf16[1024,3200]{1,0:T(8,128)(2,1)} %pad_maximum_fusion) | data formatting | bytes 13107200 | tf_op jit(solution)/shard_map/concatenate | solution.py:18
  118.9 9.5 %copy.25 = bf16[1024,25,128]{2,0,1:T(8,128)(2,1)} copy(bf16[1024,25,128]{0,2,1:T(8,128)(2,1)} %bitcast.117) | data formatting | bytes 13107200 | tf_op jit(solution)/shard_map/reshape | solution.py:37
  128.4 0.0 slice-start
  128.4 0.0 slice-start.1
  128.4 5.2 %fusion.41 = f32[9,17,128,128]{3,2,1,0:T(8,128)S(1)} fusion(bf16[25,1024,128]{2,1,0:T(8,128)(2,1)} %bitcast.97), kind=kOutput, calls=%fused_computation.46 | convolution fusion | flops 561512448 | bytes 9887744 | tf_op jit(solution)/shard_map/rti,rtj->rij/dot_general | solution.py:49
  133.6 0.0 slice-done
  133.6 0.3 slice-done.1
  133.9 1.4 fusion.95
  135.3 1.5 fusion.47
  136.8 1.5 fusion.53
  138.3 1.5 fusion.59
  139.8 1.5 fusion.65
  141.3 1.5 fusion.71
  142.8 1.5 fusion.77
  144.3 1.7 fusion.83
  146.1 1.5 fusion.89
  147.6 0.0 copy-start.1
  147.6 1.4 fusion.101
  149.0 2.3 %copy-done.1 = f32[9,17,128,128]{3,2,1,0:T(8,128)} copy-done((f32[9,17,128,128]{3,2,1,0:T(8,128)}, f32[9,17,128,128]{3,2,1,0:T(8,128)S(1)}, u32[]{:S(2)}) %copy-start.1) | copy-done | bytes 10027032
  151.3 1.4 fusion.107
  152.8 1.4 fusion.113
  154.2 1.4 fusion.119
  155.6 1.4 fusion.125
  157.0 1.4 fusion.131
  158.5 1.7 fusion.137
  160.2 1.4 fusion.143
  161.6 0.0 copy-start
  161.6 3.8 %copy-done = f32[9,17,128,128]{3,2,1,0:T(8,128)} copy-done((f32[9,17,128,128]{3,2,1,0:T(8,128)}, f32[9,17,128,128]{3,2,1,0:T(8,128)S(1)}, u32[]{:S(2)}) %copy-start) | copy-done | bytes 10027032
  165.4 7.6 %gather_fusion.1 = f32[96,128,128]{2,1,0:T(8,128)} fusion(f32[153,128,128]{2,1,0:T(8,128)} %bitcast.119, s32[1024]{0:T(1024)} %pad_clamp_fusion), kind=kCustom, calls=%fused_computation.1.clone | custom fusion | bytes 12583296 | tf_op jit(solution)/shard_map/jit(_take)/gather | solution.py:63
  173.0 0.0 copy-start.2
  173.0 7.6 %gather_fusion = f32[96,128,128]{2,1,0:T(8,128)} fusion(f32[153,128,128]{2,1,0:T(8,128)} %bitcast.118, s32[1024]{0:T(1024)} %pad_clamp_fusion), kind=kCustom, calls=%fused_computation.clone | custom fusion | bytes 12583296 | tf_op jit(solution)/shard_map/jit(_take)/gather | solution.py:62
  180.6 0.0 copy-done.2
  180.7 9.1 %select_multiply_fusion = (f32[96,128,128]{2,1,0:T(8,128)}, f32[96,128,128]{2,1,0:T(8,128)}) fusion(f32[96,128,128]{2,1,0:T(8,128)} %gather_fusion.1, pred[96]{0:T(512)(128)(4,1)S(1)} %copy-done.2, f32[96,128,128]{2,1,0:T(8,128)} %gather_fusion), kind=kLoop, calls=%fused_computation.7 | loop fusion | flops 6291456 | bytes 25165920 | tf_op jit(solution)/shard_map/div | solution.py:63
  (2 shorter events, 0.0 us)
Async XLA Ops:
  56.4 13.9 %copy-start.3 = (s32[96,2]{0,1:T(2,128)S(1)}, s32[96,2]{0,1:T(2,128)}, u32[]{:S(2)}) copy-start(s32[96,2]{0,1:T(2,128)} %param.5) | copy-start | bytes 2308
  59.0 45.4 %collective-permute-start = (bf16[1024,768]{1,0:T(8,128)(2,1)}, bf16[1024,768]{1,0:T(8,128)(2,1)}, u32[]{:S(2)}, u32[]{:S(2)}) collective-permute-start(bf16[1024,768]{1,0:T(8,128)(2,1)} %get-tuple-element.5), channel_id=1, source_target_pairs={{0,1},{1,2},{2,3},{3,4},{4,5},{5,6},{6,7},{7,8},{8,9},{9,10},{10,1... | collective-permute-start | bytes 4718600 | tf_op jit(solution)/shard_map/ppermute | solution.py:20
  60.9 43.5 %collective-permute-start.1 = (bf16[1024,768]{1,0:T(8,128)(2,1)}, bf16[1024,768]{1,0:T(8,128)(2,1)}, u32[]{:S(2)}, u32[]{:S(2)}) collective-permute-start(bf16[1024,768]{1,0:T(8,128)(2,1)} %get-tuple-element.6), channel_id=1, source_target_pairs={{1,0},{2,1},{3,2},{4,3},{5,4},{6,5},{7,6},{8,7},{9,8},{10,9},{11,1... | collective-permute-start | bytes 4718600 | tf_op jit(solution)/shard_map/ppermute | solution.py:22
  128.4 5.2 %slice-start = ((s8[6553600]{0:T(1024)(128)(4,1)}), s8[4194304]{0:T(1024)(128)(4,1)S(1)}, s32[]{:S(2)}) async-start(s8[6553600]{0:T(1024)(128)(4,1)} %bitcast.98), calls=%async_computation.1 | async-start | bytes 8388608
  128.4 5.5 %slice-start.1 = ((s8[6553600]{0:T(1024)(128)(4,1)}), s8[2359296]{0:T(1024)(128)(4,1)S(1)}, s32[]{:S(2)}) async-start(s8[6553600]{0:T(1024)(128)(4,1)} %bitcast.98), calls=%async_computation.2 | async-start | bytes 4718592
  147.6 3.8 %copy-start.1 = (f32[9,17,128,128]{3,2,1,0:T(8,128)}, f32[9,17,128,128]{3,2,1,0:T(8,128)S(1)}, u32[]{:S(2)}) copy-start(f32[9,17,128,128]{3,2,1,0:T(8,128)S(1)} %fusion.89) | copy-start | bytes 30081028
  161.6 3.8 %copy-start = (f32[9,17,128,128]{3,2,1,0:T(8,128)}, f32[9,17,128,128]{3,2,1,0:T(8,128)S(1)}, u32[]{:S(2)}) copy-start(f32[9,17,128,128]{3,2,1,0:T(8,128)S(1)} %fusion.143) | copy-start | bytes 30081028
  173.0 7.6 %copy-start.2 = (pred[96]{0:T(512)(128)(4,1)S(1)}, pred[96]{0:T(512)(128)(4,1)}, u32[]{:S(2)}) copy-start(pred[96]{0:T(512)(128)(4,1)} %get-tuple-element.3) | copy-start | bytes 292
where the time goes:
time: 191 us; the launch traced here: 190 us
  blocking collectives  55.3 us (29%)
  local copies, waits for them, and re-layouts  42.6 us (22%)
  waiting for transfers between devices  32.9 us (17%)
  matrix products  30.4 us (16%)
  other arithmetic  16.4 us (9%)
  starting transfers between devices  11.3 us (6%)
    all_to_all x1, blocking collectives, per_device(): lax.all_to_all(trajectory, ('frames', 'feat'), split_axis=1, concat_axis=...  55.3 us
    ppermute x1, waiting for transfers between devices, extended(): lax.ppermute(tail, axis, [(i, (i + 1) % count) for i in range(ends)])  32.9 us
    dot_general x9, matrix products, per_device(): jnp.einsum('rti,rtj->rij', row_panels[:, :frame_total - LAG], col_panels[...  17.4 us
    dot_general x9, matrix products, per_device(): jnp.einsum('rti,rtj->rij', row_panels, col_panels, preferred_element_type...  13 us
    concatenate x1, local copies, waits for them, and re-layouts, extended(): jnp.concatenate([lax.ppermute(tail, axis, [(i, (i + 1) % count) for i in...  9.57 us
    reshape x1, local copies, waits for them, and re-layouts, per_device(): window.reshape(frame_total, blocks_here + 2 * margin, BS).transpose(1, 0, 2)  9.51 us
    ppermute x1, starting transfers between devices, extended(): lax.ppermute(head, axis, [((i + 1) % count, i) for i in range(ends)])  9.37 us
    div x1, other arithmetic, per_device(): lagged = jnp.take(lagged_all, position, axis=0) / (frame_total - LAG)  9.07 us
  transfers between devices with their start and end apart: 2, of which 1 were waited for; matrix products, arithmetic and copies ran while one was open for 1% of the time, Pallas kernels for 0%

commit v1 on v0

v1 whole, which is shorter than its diff:
```python
import functools

import jax
import jax.numpy as jnp
from jax import lax
from jax.experimental import pallas as pl
from jax.experimental.pallas import tpu as pltpu
from jax.sharding import PartitionSpec as P

BS = 128
LAG = 16
BAND = 4
REACH = 2
MARGIN = REACH + BAND
SPAN = 2 * BAND + 1
EDGE = MARGIN + BAND
ROWS = REACH + BAND
AXES = ("frames", "feat")
F32 = jnp.float32
BF16 = jnp.bfloat16


def pair_into(pair_ref, slot, panel):
    frames = panel.shape[0]
    pair_ref[slot, :, :BS] = panel
    pair_ref[slot, : frames - LAG, BS:] = panel[LAG:]
    pair_ref[slot, frames - LAG :, BS:] = jnp.zeros((LAG, BS), BF16)


def send_tiles(place_ref, res_i, res_l, out_i, out_l, sems):
    tiles = place_ref.shape[0]

    def copies(k):
        at = place_ref[k]
        return (
            pltpu.make_async_copy(res_i.at[at], out_i.at[k], sems.at[k, 0]),
            pltpu.make_async_copy(res_l.at[at], out_l.at[k], sems.at[k, 1]),
        )

    @pl.loop(0, tiles)
    def _(k):
        @pl.when(place_ref[k] >= 0)
        def _():
            for copy in copies(k):
                copy.start()

    @pl.loop(0, tiles)
    def _(k):
        @pl.when(place_ref[k] >= 0)
        def _():
            for copy in copies(k):
                copy.wait()


def inner_kernel(blocks, place_ref, left_ref, mid_ref, right_ref, out_i, out_l, turned, pair, res_i, res_l, sems):
    frames = left_ref.shape[0]
    wide = left_ref.shape[1] // BS
    for b in range(blocks):
        if b < wide:
            panel = left_ref[:, b * BS : (b + 1) * BS]
        elif b < blocks - wide:
            panel = mid_ref[:, (b - wide) * BS : (b - wide + 1) * BS]
        else:
            c = b - (blocks - wide)
            panel = right_ref[:, c * BS : (c + 1) * BS]
        turned[b * BS : (b + 1) * BS, :] = panel.T
        pair_into(pair, b, panel)

    @pl.loop(0, blocks)
    def _(j):
        first = jnp.clip(j - BAND, 0, blocks - SPAN)
        for i in range(SPAN):
            rows = turned[pl.ds(pl.multiple_of((first + i) * BS, BS), BS), :]
            prod = jnp.dot(rows, pair[j], preferred_element_type=F32)
            res_i[j * SPAN + i] = prod[:, :BS] * (1.0 / (frames - 1))
            res_l[j * SPAN + i] = prod[:, BS:] * (1.0 / (frames - LAG))

    send_tiles(place_ref, res_i, res_l, out_i, out_l, sems)


def edge_kernel(
    place_ref, from_left, left_ref, right_ref, from_right, in_i, in_l, out_i, out_l, turned, pair, res_i, res_l, sems
):
    del in_i, in_l
    frames = left_ref.shape[0]

    def block(ref, b):
        return ref[:, b * BS : (b + 1) * BS]

    wide = left_ref.shape[1] // BS
    for side in range(2):
        if side == 0:
            cols = [block(from_left, b) for b in range(MARGIN)] + [block(left_ref, b) for b in range(BAND)]
            row0 = MARGIN - REACH
        else:
            cols = [block(right_ref, wide - BAND + b) for b in range(BAND)] + [block(from_right, b) for b in range(MARGIN)]
            row0 = 0
        for r in range(ROWS):
            turned[r * BS : (r + 1) * BS, :] = cols[row0 + r].T
        for c in range(EDGE):
            pair_into(pair, c, cols[c])
        for c in range(EDGE):
            if side == 0:
                own_col = c >= MARGIN
                keep = [r for r in range(ROWS) if abs(r + row0 - c) <= BAND and (r < REACH or not own_col)]
            else:
                own_col = c < BAND
                keep = [r for r in range(ROWS) if abs(r + row0 - c) <= BAND and (r >= BAND or not own_col)]
            lo, hi = keep[0], keep[-1] + 1
            prod = jnp.dot(turned[lo * BS : hi * BS, :], pair[c], preferred_element_type=F32)
            for r in range(lo, hi):
                part = prod[(r - lo) * BS : (r - lo + 1) * BS]
                at = side * ROWS * EDGE + r * EDGE + c
                res_i[at] = part[:, :BS] * (1.0 / (frames - 1))
                res_l[at] = part[:, BS:] * (1.0 / (frames - LAG))

    send_tiles(place_ref, res_i, res_l, out_i, out_l, sems)


def per_device(trajectory, tile_list):
    panels = lax.all_to_all(trajectory, AXES, split_axis=1, concat_axis=0, tiled=True)
    frames = panels.shape[0]
    blocks = panels.shape[1] // BS
    tiles = tile_list.shape[0]
    count = lax.axis_size(AXES)

    rel = tile_list - lax.axis_index(AXES) * blocks
    row, col = rel[:, 0], rel[:, 1]
    on_left = (row < 0) | (col < 0)
    on_right = (row >= blocks) | (col >= blocks)
    inner_place = jnp.where(on_left | on_right, -1, col * SPAN + row - jnp.clip(col - BAND, 0, blocks - SPAN))
    left_place = (row + REACH) * EDGE + col + MARGIN
    right_place = ROWS * EDGE + (row - (blocks - BAND)) * EDGE + col - (blocks - BAND)
    edge_place = jnp.where(on_left, left_place, jnp.where(on_right, right_place, -1))

    column_means = jnp.sum(panels, axis=0, dtype=F32) / frames

    def centred(lo, hi):
        return (panels[:, lo * BS : hi * BS] - column_means[lo * BS : hi * BS]).astype(BF16)

    left = centred(0, MARGIN)
    right = centred(blocks - MARGIN, blocks)
    mid = centred(MARGIN, blocks - MARGIN)
    from_right = lax.ppermute(left, AXES, [(i + 1, i) for i in range(count - 1)])
    from_left = lax.ppermute(right, AXES, [(i, i + 1) for i in range(count - 1)])

    vmem = pl.BlockSpec(memory_space=pltpu.VMEM)
    smem = pl.BlockSpec(memory_space=pltpu.SMEM)
    hbm = pl.BlockSpec(memory_space=pl.ANY)
    outs = [jax.ShapeDtypeStruct((tiles, BS, BS), F32)] * 2
    inner = pl.pallas_call(
        functools.partial(inner_kernel, blocks),
        out_shape=outs,
        in_specs=[smem, vmem, vmem, vmem],
        out_specs=[hbm, hbm],
        scratch_shapes=[
            pltpu.VMEM((blocks * BS, frames), BF16),
            pltpu.VMEM((blocks, frames, 2 * BS), BF16),
            pltpu.VMEM((blocks * SPAN, BS, BS), F32),
            pltpu.VMEM((blocks * SPAN, BS, BS), F32),
            pltpu.SemaphoreType.DMA((tiles, 2)),
        ],
        compiler_params=pltpu.CompilerParams(vmem_limit_bytes=44 << 20),
        cost_estimate=pl.CostEstimate(
            flops=2 * blocks * SPAN * BS * BS * frames * 2, bytes_accessed=16 << 20, transcendentals=0
        ),
        name="inner_tiles",
    )
    inst, lagg = inner(inner_place, left, mid, right)
    edge = pl.pallas_call(
        edge_kernel,
        out_shape=outs,
        in_specs=[smem, vmem, vmem, vmem, vmem, hbm, hbm],
        out_specs=[hbm, hbm],
        scratch_shapes=[
            pltpu.VMEM((ROWS * BS, frames), BF16),
            pltpu.VMEM((EDGE, frames, 2 * BS), BF16),
            pltpu.VMEM((2 * ROWS * EDGE, BS, BS), F32),
            pltpu.VMEM((2 * ROWS * EDGE, BS, BS), F32),
            pltpu.SemaphoreType.DMA((tiles, 2)),
        ],
        input_output_aliases={5: 0, 6: 1},
        compiler_params=pltpu.CompilerParams(vmem_limit_bytes=44 << 20),
        cost_estimate=pl.CostEstimate(
            flops=2 * 56 * BS * BS * frames * 2, bytes_accessed=16 << 20, transcendentals=0
        ),
        name="edge_tiles",
    )
    inst, lagg = edge(edge_place, from_left, left, right, from_right, inst, lagg)
    return (inst, lagg)


def solution(mesh):
    in_specs = (P(AXES, None), P(AXES, None))
    out_specs = (P(AXES, None, None), P(AXES, None, None))
    return jax.shard_map(per_device, mesh=mesh, in_specs=in_specs, out_specs=out_specs, check_vma=False)
```

time: 191 us -> 118 us (0.62)
  local copies, waits for them, and re-layouts: 42.6 us -> 0.49 us
  matrix products: 30.4 us -> 0 us
  Pallas kernels: 0 us -> 27.6 us
  other arithmetic: 16.4 us -> 2.27 us
  waiting for transfers between devices: 32.9 us -> 23.4 us
  starting transfers between devices: 11.3 us -> 7.86 us
    dot_general x18 -> x0, matrix products: 30.4 us -> none  [the longest x9 17.4 us: per_device(): jnp.einsum('rti,rtj->rij', row_panels[:, :frame_total - LAG], col_panels[...]
    pallas_call x0 -> x2, Pallas kernels: none -> 27.6 us  [the longest x1 16.7 us: per_device(): inst, lagg = inner(inner_place, left, mid, right)]
    gather x2 -> x0, local copies, waits for them, and re-layouts: 15.2 us -> none  [the longest x1 7.62 us: per_device(): instant = jnp.take(instant_all, position, axis=0) / (frame_total - 1)]
    concatenate x1 -> x0, local copies, waits for them, and re-layouts: 9.57 us -> none  [extended(): jnp.concatenate([lax.ppermute(tail, axis, [(i, (i + 1) % count) for i in...]
    reshape x1 -> x0, local copies, waits for them, and re-layouts: 9.51 us -> none  [per_device(): window.reshape(frame_total, blocks_here + 2 * margin, BS).transpose(1, 0, 2)]
    ppermute x2, waiting for transfers between devices: 32.9 us -> 23.4 us  [the longest x1 12.2 us: per_device(): lax.ppermute(right, AXES, [(i, i + 1) for i in range(count - 1)])]
    div x2 -> x1, other arithmetic: 9.07 us -> 0.01 us  [per_device(): column_means = jnp.sum(panels, axis=0, dtype=F32) / frames]
    unnamed x12 -> x4, local copies, waits for them, and re-layouts: 6.45 us -> 0.48 us
  transfers between devices with their start and end apart: 2 -> 2, of which waited for: 1 -> 2; matrix products, arithmetic and copies ran while one was open for 1% -> 1% of each run, Pallas kernels for 0% -> 14%
where the time goes in v1:
time: 118 us
  blocking collectives  55.3 us (47%)
  Pallas kernels  27.6 us (23%)
  waiting for transfers between devices  23.4 us (20%)
  starting transfers between devices  7.86 us (7%)
  other arithmetic  2.27 us (2%)
    all_to_all x1, blocking collectives, per_device(): lax.all_to_all(trajectory, AXES, split_axis=1, concat_axis=0, tiled=True)  55.3 us
    pallas_call x1, Pallas kernels, per_device(): inst, lagg = inner(inner_place, left, mid, right)  16.7 us
    ppermute x1, waiting for transfers between devices, per_device(): lax.ppermute(right, AXES, [(i, i + 1) for i in range(count - 1)])  12.2 us
    ppermute x1, waiting for transfers between devices, per_device(): lax.ppermute(left, AXES, [(i + 1, i) for i in range(count - 1)])  11.3 us
    pallas_call x1, Pallas kernels, per_device(): edge(edge_place, from_left, left, right, from_right, inst, lagg)  10.9 us
    ppermute x1, starting transfers between devices, per_device(): lax.ppermute(left, AXES, [(i + 1, i) for i in range(count - 1)])  5.94 us
  transfers between devices with their start and end apart: 2, of which 2 were waited for; matrix products, arithmetic and copies ran while one was open for 1% of the time, Pallas kernels for 14%

profile of v1, /device:TPU:1, one launch (start us, length us, event | category | flops | bytes accessed | tf_op | source)
XLA Modules:
  0.0 117.6 jit_solution(1259868996149272848)
XLA Ops:
  0.6 55.3 %all_to_all.19 = bf16[8,128,1664]{2,0,1:T(8,128)(2,1)S(1)} all-to-all(bf16[8,128,1664]{2,0,1:T(8,128)(2,1)} %bitcast.66), channel_id=1, replica_groups=mesh['frames'=4,'feat'=32] {'frames','feat'}, dimensions={1} | all-to-all | bytes 6815744 | tf_op jit(solution)/shard_map/all_to_all | solution.py:121
  55.9 0.0 copy-start
  55.9 0.5 convert_reduce_fusion
  56.5 0.0 copy-start.1
  56.5 0.7 subtract_convert_fusion
  57.2 0.5 copy-done
  57.7 5.9 %collective-permute-start.1 = (bf16[1024,768]{1,0:T(8,128)(2,1)S(1)}, bf16[1024,768]{1,0:T(8,128)(2,1)}, u32[]{:S(2)}, u32[]{:S(2)}) collective-permute-start(bf16[1024,768]{1,0:T(8,128)(2,1)S(1)} %get-tuple-element.6.left_ref), channel_id=1, source_target_pairs={{1,0},{2,1},{3,2},{4,3},{5,4},{6,5},{7,6},{8,7},{9,8},{10,9},{11,1... | collective-permute-start | bytes 4718600 | tf_op jit(solution)/shard_map/ppermute | solution.py:144
  63.6 1.9 %collective-permute-start = (bf16[1024,768]{1,0:T(8,128)(2,1)S(1)}, bf16[1024,768]{1,0:T(8,128)(2,1)}, u32[]{:S(2)}, u32[]{:S(2)}) collective-permute-start(bf16[1024,768]{1,0:T(8,128)(2,1)S(1)} %get-tuple-element.7.right_ref), channel_id=1, source_target_pairs={{0,1},{1,2},{2,3},{3,4},{4,5},{5,6},{6,7},{7,8},{8,9},{9,10},{10,1... | collective-permute-start | bytes 4718600 | tf_op jit(solution)/shard_map/ppermute | solution.py:145
  65.5 0.0 copy-done.1
  65.6 1.0 subtract_convert_fusion.2.mid_ref
  66.6 16.7 %inner_tiles.1 = (f32[96,128,128]{2,1,0:T(8,128)}, f32[96,128,128]{2,1,0:T(8,128)}) custom-call(s32[96]{0:T(128)S(1)} %get-tuple-element.10.place_ref, bf16[1024,768]{1,0:T(8,128)(2,1)S(1)} %get-tuple-element.6.left_ref, bf16[1024,128]{1,0:T(8,128)(2,1)S(1)} %subtract_convert_fusion.2.mid_ref, bf16[1024,768]{1,0:T(8,128)(2,1)S(1)} %get-tuple-element.7.right_ref), custom_call_target="tpu_custom_call" | custom-call | flops 7851737088 | bytes 16777216 | tf_op jit(solution)/shard_map/inner_tiles/pallas_call | solution.py:169
  83.3 11.3 %collective-permute-done.1.from_right = bf16[1024,768]{1,0:T(8,128)(2,1)} collective-permute-done((bf16[1024,768]{1,0:T(8,128)(2,1)S(1)}, bf16[1024,768]{1,0:T(8,128)(2,1)}, u32[]{:S(2)}, u32[]{:S(2)}) %collective-permute-start.1) | collective-permute-done | bytes 1572896 | tf_op jit(solution)/shard_map/ppermute | solution.py:144
  94.6 12.2 %collective-permute-done.from_left = bf16[1024,768]{1,0:T(8,128)(2,1)} collective-permute-done((bf16[1024,768]{1,0:T(8,128)(2,1)S(1)}, bf16[1024,768]{1,0:T(8,128)(2,1)}, u32[]{:S(2)}, u32[]{:S(2)}) %collective-permute-start) | collective-permute-done | bytes 1572896 | tf_op jit(solution)/shard_map/ppermute | solution.py:145
  106.7 10.9 %edge_tiles.1 = (f32[96,128,128]{2,1,0:T(8,128)}, f32[96,128,128]{2,1,0:T(8,128)}) custom-call(s32[96]{0:T(128)S(1)} %get-tuple-element.11.place_ref, bf16[1024,768]{1,0:T(8,128)(2,1)} %collective-permute-done.from_left, bf16[1024,768]{1,0:T(8,128)(2,1)S(1)} %get-tuple-element.6.left_ref, ...), custom_call_target="tpu_custom_call", output_to_operand_aliasing={{0}: (5, {}), {1}: (6, {})} | custom-call | flops 3758096384 | bytes 16777216 | tf_op jit(solution)/shard_map/edge_tiles/pallas_call | solution.py:189
  (5 shorter events, 0.0 us)
Async XLA Ops:
  55.9 1.8 %copy-start = (bf16[8,128,1664]{2,0,1:T(8,128)(2,1)}, bf16[8,128,1664]{2,0,1:T(8,128)(2,1)S(1)}, u32[]{:S(2)}) copy-start(bf16[8,128,1664]{2,0,1:T(8,128)(2,1)S(1)} %all_to_all.19) | copy-start | bytes 10223620
  56.5 9.1 %copy-start.1 = (s32[96,2]{0,1:T(2,128)S(1)}, s32[96,2]{0,1:T(2,128)}, u32[]{:S(2)}) copy-start(s32[96,2]{0,1:T(2,128)} %param.3) | copy-start | bytes 2308
  57.7 36.9 %collective-permute-start.1 = (bf16[1024,768]{1,0:T(8,128)(2,1)S(1)}, bf16[1024,768]{1,0:T(8,128)(2,1)}, u32[]{:S(2)}, u32[]{:S(2)}) collective-permute-start(bf16[1024,768]{1,0:T(8,128)(2,1)S(1)} %get-tuple-element.6.left_ref), channel_id=1, source_target_pairs={{1,0},{2,1},{3,2},{4,3},{5,4},{6,5},{7,6},{8,7},{9,8},{10,9},{11,1... | collective-permute-start | bytes 4718600 | tf_op jit(solution)/shard_map/ppermute | solution.py:144
  63.6 43.1 %collective-permute-start = (bf16[1024,768]{1,0:T(8,128)(2,1)S(1)}, bf16[1024,768]{1,0:T(8,128)(2,1)}, u32[]{:S(2)}, u32[]{:S(2)}) collective-permute-start(bf16[1024,768]{1,0:T(8,128)(2,1)S(1)} %get-tuple-element.7.right_ref), channel_id=1, source_target_pairs={{0,1},{1,2},{2,3},{3,4},{4,5},{5,6},{6,7},{7,8},{8,9},{9,10},{10,1... | collective-permute-start | bytes 4718600 | tf_op jit(solution)/shard_map/ppermute | solution.py:145

commit v2 on v0

v2 whole, which is shorter than its diff:
```python
import functools

import jax
import jax.numpy as jnp
from jax import lax
from jax.experimental import pallas as pl
from jax.experimental.pallas import tpu as pltpu
from jax.sharding import PartitionSpec as P

BS = 128
LAG = 16
BAND = 4
REACH = 2
HALO = 4
SPAN = 2 * BAND + 1
ROWS = REACH + BAND
COLS = HALO + BAND
SLOT = 128
AXES = ("frames", "feat")
F32 = jnp.float32
BF16 = jnp.bfloat16
VMEM = pl.BlockSpec(memory_space=pltpu.VMEM)
SMEM = pl.BlockSpec(memory_space=pltpu.SMEM)
HBM = pl.BlockSpec(memory_space=pl.ANY)


def far_tiles(blocks):
    low, high = [], []
    for col in range(HALO, REACH + BAND):
        low.append((col, list(range(max(0, col - BAND), REACH))))
    for col in range(blocks - 1 - HALO, blocks - 1 - REACH - BAND, -1):
        high.append((col, list(range(blocks - REACH, min(blocks, col + BAND + 1)))))
    return low, high


def far_count():
    reach = REACH + BAND - HALO
    return reach * (reach + 1) // 2


def centred(panels_ref, b):
    panel = panels_ref[:, b * BS : (b + 1) * BS].astype(F32)
    mean = jnp.sum(panel, axis=0, keepdims=True) * (1.0 / panel.shape[0])
    return (panel - mean).astype(BF16)


def pair_into(pair_ref, slot, panel):
    frames = panel.shape[0]
    pair_ref[slot, :, :BS] = panel
    pair_ref[slot, : frames - LAG, BS:] = panel[LAG:]
    pair_ref[slot, frames - LAG :, BS:] = jnp.zeros((LAG, BS), BF16)


def block_rows(first, last):
    return slice(first * BS, last * BS)


def copies(key, res, out_i, out_l, sems, base):
    at = lax.shift_right_logical(key, 7) - base
    tile = lax.bitwise_and(key, SLOT - 1)
    return (
        pltpu.make_async_copy(res.at[at, 0], out_i.at[tile], sems.at[tile, 0]),
        pltpu.make_async_copy(res.at[at, 1], out_l.at[tile], sems.at[tile, 1]),
    )


def start_run(keys_ref, first, last, *where):
    @pl.loop(first, last)
    def _(r):
        for copy in copies(keys_ref[r], *where):
            copy.start()


def wait_run(keys_ref, first, last, *where):
    @pl.loop(first, last)
    def _(r):
        for copy in copies(keys_ref[r], *where):
            copy.wait()


def keep(res, at, part, frames):
    res[at, 0] = part[:, :BS] * (1.0 / (frames - 1))
    res[at, 1] = part[:, BS:] * (1.0 / (frames - LAG))


def far_kernel(blocks, own_ref, low_ref, high_ref, turned, pair):
    frames = own_ref.shape[0]
    scale = jnp.where(lax.broadcasted_iota(jnp.int32, (1, 2 * BS), 1) < BS, 1.0 / (frames - 1), 1.0 / (frames - LAG))
    for side, out_ref in zip(far_tiles(blocks), (low_ref, high_ref)):
        first = min(rows[0] for _, rows in side)
        for row in sorted({row for _, rows in side for row in rows}):
            turned[block_rows(row - first, row - first + 1), :] = centred(own_ref, row).T
        at = 0
        for slot, (col, rows) in enumerate(side):
            pair_into(pair, slot, centred(own_ref, col))
            lhs = turned[block_rows(rows[0] - first, rows[-1] + 1 - first), :]
            prod = jnp.dot(lhs, pair[slot], preferred_element_type=F32)
            out_ref[block_rows(at, at + len(rows)), :] = (prod * scale).astype(BF16)
            at += len(rows)


def inner_kernel(
    blocks, groups, keys_ref, ends_ref, own_ref, out_i, out_l, rows_l, rows_r, cols_l, cols_r, turned, pair, res, sems, side_sems
):
    frames = own_ref.shape[0]
    where = (res, out_i, out_l, sems, 0)
    far = blocks - BAND
    side_copies = [
        pltpu.make_async_copy(turned.at[pl.ds(0, BAND * BS)], rows_l, side_sems.at[0]),
        pltpu.make_async_copy(turned.at[pl.ds(far * BS, BAND * BS)], rows_r, side_sems.at[1]),
        pltpu.make_async_copy(pair.at[pl.ds(0, BAND)], cols_l, side_sems.at[2]),
        pltpu.make_async_copy(pair.at[pl.ds(far, BAND)], cols_r, side_sems.at[3]),
    ]
    ready = 0
    first = 0
    for end in groups:
        for b in range(ready, min(blocks, end + BAND)):
            panel = centred(own_ref, b)
            turned[block_rows(b, b + 1), :] = panel.T
            pair_into(pair, b, panel)
        if ready < blocks <= end + BAND:
            for copy in side_copies:
                copy.start()
        ready = min(blocks, end + BAND)
        for col in range(first, end):
            low, high = max(0, col - BAND), min(blocks, col + BAND + 1)
            prod = jnp.dot(turned[block_rows(low, high), :], pair[col], preferred_element_type=F32)
            for row in range(low, high):
                keep(res, col * SPAN + row - col + BAND, prod[block_rows(row - low, row - low + 1)], frames)
        start_run(keys_ref, ends_ref[first], ends_ref[end], *where)
        first = end
    for copy in side_copies:
        copy.wait()
    wait_run(keys_ref, 0, ends_ref[blocks], *where)


def edge_kernel(
    blocks, base, keys_ref, ends_ref, far_l, far_r, rows_l, rows_r, cols_l, cols_r, halo_ref, in_i, in_l,
    out_i, out_l, raw, far, turned, pair, res, sems, in_sems,
):
    del in_i, in_l
    frames = halo_ref.shape[0]
    where = (res, out_i, out_l, sems, base)
    count = far_count()
    halo0, own0, row0 = (0, BAND), (HALO, 0), (HALO - REACH, 0)

    def halo_copy(side, b):
        at = side * HALO + b
        return pltpu.make_async_copy(halo_ref.at[:, pl.ds(at * BS, BS)], raw.at[at], in_sems.at[at])

    def side_copy(side, kind):
        src, dst = (
            ((far_l, far_r)[side], far.at[side]),
            ((rows_l, rows_r)[side], turned.at[side, pl.ds((own0[side] - row0[side]) * BS, BAND * BS)]),
            ((cols_l, cols_r)[side], pair.at[side, pl.ds(own0[side], BAND)]),
        )[kind]
        return pltpu.make_async_copy(src, dst, in_sems.at[2 * HALO + 3 * side + kind])

    for side in range(2):
        for b in range(HALO):
            halo_copy(side, b).start()
        for kind in (1, 2, 0):
            side_copy(side, kind).start()
    for side in range(2):
        for b in range(HALO):
            halo_copy(side, b).wait()
            panel = centred(raw.at[side * HALO + b], 0)
            pair_into(pair.at[side], halo0[side] + b, panel)
            row = halo0[side] + b - row0[side]
            if 0 <= row < ROWS:
                turned[side, block_rows(row, row + 1), :] = panel.T
        side_copy(side, 1).wait()
        side_copy(side, 2).wait()
        for col in range(COLS):
            rows = [row for row in range(ROWS) if abs(row + row0[side] - col) <= BAND]
            if own0[side] <= col < own0[side] + BAND:
                rows = [row for row in rows if (row < REACH if side == 0 else row >= BAND)]
            low, high = rows[0], rows[-1] + 1
            prod = jnp.dot(turned[side, block_rows(low, high), :], pair[side, col], preferred_element_type=F32)
            for row in rows:
                at = 2 * count + (side * ROWS + row) * COLS + col
                keep(res, at, prod[block_rows(row - low, row - low + 1)], frames)
        start_run(keys_ref, ends_ref[blocks + 1 + side], ends_ref[blocks + 2 + side], *where)
        if side == 0:
            for other in range(2):
                side_copy(other, 0).wait()
                for t in range(count):
                    for half in range(2):
                        part = far[other, block_rows(t, t + 1), half * BS : (half + 1) * BS]
                        res[other * count + t, half] = part.astype(F32)
            start_run(keys_ref, ends_ref[blocks], ends_ref[blocks + 1], *where)
    wait_run(keys_ref, ends_ref[blocks], keys_ref.shape[0], *where)


def sorted_keys(tile_list, blocks):
    tiles = tile_list.shape[0]
    rel = tile_list - lax.axis_index(AXES) * blocks
    row, col = rel[:, 0], rel[:, 1]
    inner = col * SPAN + row - col + BAND
    far0 = blocks * SPAN
    reach = REACH + BAND - HALO
    below = -HALO - 1 - col
    above = col - (blocks + HALO)

    def before(step):
        return step * reach - step * (step - 1) // 2

    far_low = far0 + before(below) + row + REACH
    far_high = far0 + far_count() + before(above) + row - (blocks + HALO - BAND) - above
    left0 = far0 + 2 * far_count()
    right0 = left0 + ROWS * COLS
    left = left0 + (row + REACH) * COLS + col + HALO
    right = right0 + (row - (blocks - BAND)) * COLS + col - (blocks - BAND)
    place = jnp.where((row >= blocks) | (col >= blocks), right, inner)
    place = jnp.where((row < 0) | (col < 0), left, place)
    place = jnp.where(below >= 0, far_low, jnp.where(above >= 0, far_high, place))
    key = place * SLOT + lax.iota(jnp.int32, tiles)
    rank = jnp.sum((key[None, :] < key[:, None]).astype(jnp.int32), axis=1)
    keys = jnp.sum(jnp.where(rank[None, :] == lax.iota(jnp.int32, tiles)[:, None], key[None, :], 0), axis=1)
    number = lax.iota(jnp.int32, blocks + 4)
    edges = number * SPAN
    for at, value in ((1, left0), (2, right0), (3, right0 + ROWS * COLS)):
        edges = jnp.where(number == blocks + at, value, edges)
    ends = jnp.sum((key[None, :] < edges[:, None] * SLOT).astype(jnp.int32), axis=1)
    return keys, ends, far0


def per_device(trajectory, tile_list):
    count = lax.axis_size(AXES)
    parts = trajectory.reshape(trajectory.shape[0], count, -1)
    blocks = parts.shape[2] // BS
    tiles = tile_list.shape[0]
    own = lax.all_to_all(trajectory, AXES, split_axis=1, concat_axis=0, tiled=True)
    frames = own.shape[0]
    edge = HALO * BS
    beside = jnp.concatenate(
        [
            jnp.pad(parts[:, :-1, parts.shape[2] - edge :], ((0, 0), (1, 0), (0, 0))),
            jnp.pad(parts[:, 1:, :edge], ((0, 0), (0, 1), (0, 0))),
        ],
        axis=2,
    )
    keys, ends, base = sorted_keys(tile_list, blocks)
    own, beside, keys, ends = lax.optimization_barrier((own, beside, keys, ends))
    halo = lax.all_to_all(beside, AXES, split_axis=1, concat_axis=0, tiled=True).reshape(frames, 2 * edge)

    low, high = far_tiles(blocks)
    far = far_count()
    to_left, to_right = pl.pallas_call(
        functools.partial(far_kernel, blocks),
        out_shape=[jax.ShapeDtypeStruct((far * BS, 2 * BS), BF16)] * 2,
        in_specs=[VMEM],
        out_specs=[VMEM, VMEM],
        scratch_shapes=[
            pltpu.VMEM((REACH * BS, frames), BF16),
            pltpu.VMEM((len(low), frames, 2 * BS), BF16),
        ],
        compiler_params=pltpu.CompilerParams(vmem_limit_bytes=16 << 20),
        cost_estimate=pl.CostEstimate(flops=2 * far * 4 * BS * BS * frames, bytes_accessed=6 << 20, transcendentals=0),
        name="far_tiles",
    )(own)
    far_r = lax.ppermute(to_left, AXES, [(i + 1, i) for i in range(count - 1)])
    far_l = lax.ppermute(to_right, AXES, [(i, i + 1) for i in range(count - 1)])

    outs = [jax.ShapeDtypeStruct((tiles, BS, BS), F32)] * 2
    inst, lagg, rows_l, rows_r, cols_l, cols_r = pl.pallas_call(
        functools.partial(inner_kernel, blocks, (blocks,)),
        out_shape=outs
        + [jax.ShapeDtypeStruct((BAND * BS, frames), BF16)] * 2
        + [jax.ShapeDtypeStruct((BAND, frames, 2 * BS), BF16)] * 2,
        in_specs=[SMEM, SMEM, VMEM],
        out_specs=[HBM] * 6,
        scratch_shapes=[
            pltpu.VMEM((blocks * BS, frames), BF16),
            pltpu.VMEM((blocks, frames, 2 * BS), BF16),
            pltpu.VMEM((blocks * SPAN, 2, BS, BS), F32),
            pltpu.SemaphoreType.DMA((tiles, 2)),
            pltpu.SemaphoreType.DMA((4,)),
        ],
        compiler_params=pltpu.CompilerParams(vmem_limit_bytes=58 << 20),
        cost_estimate=pl.CostEstimate(
            flops=blocks * SPAN * 4 * BS * BS * frames, bytes_accessed=20 << 20, transcendentals=0
        ),
        name="inner_tiles",
    )(keys, ends, own)
    inst, lagg = pl.pallas_call(
        functools.partial(edge_kernel, blocks, base),
        out_shape=outs,
        in_specs=[SMEM, SMEM] + [HBM] * 9,
        out_specs=[HBM, HBM],
        scratch_shapes=[
            pltpu.VMEM((2 * HALO, frames, BS), BF16),
            pltpu.VMEM((2, far * BS, 2 * BS), BF16),
            pltpu.VMEM((2, ROWS * BS, frames), BF16),
            pltpu.VMEM((2, COLS, frames, 2 * BS), BF16),
            pltpu.VMEM((2 * far + 2 * ROWS * COLS, 2, BS, BS), F32),
            pltpu.SemaphoreType.DMA((tiles, 2)),
            pltpu.SemaphoreType.DMA((2 * HALO + 6,)),
        ],
        input_output_aliases={9: 0, 10: 1},
        compiler_params=pltpu.CompilerParams(vmem_limit_bytes=58 << 20),
        cost_estimate=pl.CostEstimate(flops=50 * 4 * BS * BS * frames, bytes_accessed=16 << 20, transcendentals=0),
        name="edge_tiles",
    )(keys, ends, far_l, far_r, rows_l, rows_r, cols_l, cols_r, halo, inst, lagg)
    return (inst, lagg)


def solution(mesh):
    in_specs = (P(AXES, None), P(AXES, None))
    out_specs = (P(AXES, None, None), P(AXES, None, None))
    return jax.shard_map(per_device, mesh=mesh, in_specs=in_specs, out_specs=out_specs, check_vma=False)
```

time: 191 us -> 109 us (0.57)
  blocking collectives: 55.3 us -> 0 us
  local copies, waits for them, and re-layouts: 42.6 us -> 2.42 us
  matrix products: 30.4 us -> 0 us
  Pallas kernels: 0 us -> 27.1 us
  starting transfers between devices: 11.3 us -> 29.9 us
  other arithmetic: 16.4 us -> 3.16 us
  waiting for transfers between devices: 32.9 us -> 45.2 us
    all_to_all x1 -> x0, blocking collectives: 55.3 us -> none  [per_device(): lax.all_to_all(trajectory, ('frames', 'feat'), split_axis=1, concat_axis=...]
    all_to_all x0 -> x2, waiting for transfers between devices: none -> 38.9 us  [the longest x1 38.9 us: per_device(): lax.all_to_all(trajectory, AXES, split_axis=1, concat_axis=0, tiled=True)]
    dot_general x18 -> x0, matrix products: 30.4 us -> none  [the longest x9 17.4 us: per_device(): jnp.einsum('rti,rtj->rij', row_panels[:, :frame_total - LAG], col_panels[...]
    pallas_call x0 -> x3, Pallas kernels: none -> 27.1 us  [the longest x1 14.8 us: per_device(): pl.pallas_call(functools.partial(inner_kernel, blocks, (blocks,)), out_sh...]
    ppermute x2, waiting for transfers between devices: 32.9 us -> 6.3 us  [the longest x1 6.3 us: per_device(): far_l = lax.ppermute(to_right, AXES, [(i, i + 1) for i in range(count - 1)])]
    all_to_all x0 -> x2, starting transfers between devices: none -> 18.1 us  [the longest x1 11.5 us: per_device(): lax.all_to_all(trajectory, AXES, split_axis=1, concat_axis=0, tiled=True)]
    gather x2 -> x0, local copies, waits for them, and re-layouts: 15.2 us -> none  [the longest x1 7.62 us: per_device(): instant = jnp.take(instant_all, position, axis=0) / (frame_total - 1)]
    concatenate x1 -> x0, local copies, waits for them, and re-layouts: 9.57 us -> none  [extended(): jnp.concatenate([lax.ppermute(tail, axis, [(i, (i + 1) % count) for i in...]
  transfers between devices with their start and end apart: 2 -> 4, of which waited for: 1 -> 2; matrix products, arithmetic and copies ran while one was open for 1% -> 4% of each run, Pallas kernels for 0% -> 15%
where the time goes in v2:
time: 109 us
  waiting for transfers between devices  45.2 us (41%)
  starting transfers between devices  29.9 us (27%)
  Pallas kernels  27.1 us (25%)
  other arithmetic  3.16 us (3%)
  local copies, waits for them, and re-layouts  2.42 us (2%)
    all_to_all x1, waiting for transfers between devices, per_device(): lax.all_to_all(trajectory, AXES, split_axis=1, concat_axis=0, tiled=True)  38.9 us
    pallas_call x1, Pallas kernels, per_device(): pl.pallas_call(functools.partial(inner_kernel, blocks, (blocks,)), out_sh...  14.8 us
    all_to_all x1, starting transfers between devices, per_device(): lax.all_to_all(trajectory, AXES, split_axis=1, concat_axis=0, tiled=True)  11.5 us
    pallas_call x1, Pallas kernels, per_device(): pl.pallas_call(functools.partial(edge_kernel, blocks, base), out_shape=ou...  11 us
    ppermute x1, starting transfers between devices, per_device(): far_r = lax.ppermute(to_left, AXES, [(i + 1, i) for i in range(count - 1)])  8.53 us
    all_to_all x1, starting transfers between devices, per_device(): lax.all_to_all(beside, AXES, split_axis=1, concat_axis=0, tiled=True)  6.61 us
    ppermute x1, waiting for transfers between devices, per_device(): far_l = lax.ppermute(to_right, AXES, [(i, i + 1) for i in range(count - 1)])  6.3 us
    ppermute x1, starting transfers between devices, per_device(): far_l = lax.ppermute(to_right, AXES, [(i, i + 1) for i in range(count - 1)])  3.29 us
  transfers between devices with their start and end apart: 4, of which 2 were waited for; matrix products, arithmetic and copies ran while one was open for 4% of the time, Pallas kernels for 15%

profile of v2, /device:TPU:1, one launch (start us, length us, event | category | flops | bytes accessed | tf_op | source)
XLA Modules:
  0.0 108.7 jit_solution(11522608176506788307)
XLA Ops:
  0.6 0.0 copy-start.3
  0.6 11.5 %all-to-all-start = ((bf16[8,128,1664]{2,0,1:T(8,128)(2,1)}), bf16[8,128,1664]{2,0,1:T(8,128)(2,1)S(1)}, u32[]{:S(2)}, u32[]{:S(2)}) async-start(bf16[8,128,1664]{2,0,1:T(8,128)(2,1)} %bitcast.87), calls=%async_computation | async-start | bytes 6815744 | tf_op jit(solution)/shard_map/all_to_all | solution.py:233
  12.2 0.0 copy-done.3
  12.2 0.2 convert_reduce_fusion
  12.4 0.7 select_reduce_fusion.keys_ref
  13.1 0.7 convert_reduce_fusion.1.ends_ref
  13.8 1.7 %fusion.24 = (bf16[8,127,512]{2,0,1:T(8,128)(2,1)S(1)}, bf16[8,127,512]{2,0,1:T(8,128)(2,1)S(1)}) fusion(bf16[8,128,1664]{2,0,1:T(8,128)(2,1)} %bitcast.88), kind=kLoop, calls=%fused_computation.71 | loop fusion | bytes 4161536 | tf_op jit(solution)/shard_map/slice | solution.py:238
  15.5 1.6 %fusion.2 = bf16[8,128,1024]{2,0,1:T(8,128)(2,1)} fusion(bf16[8,127,512]{2,0,1:T(8,128)(2,1)S(1)} %get-tuple-element.27, bf16[8,127,512]{2,0,1:T(8,128)(2,1)S(1)} %get-tuple-element.26), kind=kLoop, calls=%fused_computation.4 | loop fusion | flops 8388608 | bytes 4177920 | tf_op jit(solution)/shard_map/concatenate | solution.py:236
  17.0 38.9 %all-to-all-done = bf16[8,128,1664]{2,0,1:T(8,128)(2,1)S(1)} async-done(((bf16[8,128,1664]{2,0,1:T(8,128)(2,1)}), bf16[8,128,1664]{2,0,1:T(8,128)(2,1)S(1)}, u32[]{:S(2)}, u32[]{:S(2)}) %all-to-all-start) | async-done | bytes 3407904 | tf_op jit(solution)/shard_map/all_to_all | solution.py:233
  55.9 0.0 copy-start
  55.9 6.6 %all-to-all-start.1 = ((bf16[8,128,1024]{2,0,1:T(8,128)(2,1)}), bf16[8,128,1024]{2,0,1:T(8,128)(2,1)}, u32[]{:S(2)}, u32[]{:S(2)}) async-start(bf16[8,128,1024]{2,0,1:T(8,128)(2,1)} %fusion.2), calls=%async_computation.1 | async-start | bytes 4194304 | tf_op jit(solution)/shard_map/all_to_all | solution.py:245
  62.5 1.3 %far_tiles.1 = (bf16[384,256]{1,0:T(8,128)(2,1)S(1)}, bf16[384,256]{1,0:T(8,128)(2,1)S(1)}) custom-call(bf16[1024,1664]{1,0:T(8,128)(2,1)S(1)} %bitcast.85), custom_call_target="tpu_custom_call" | custom-call | flops 402653184 | bytes 6291456 | tf_op jit(solution)/shard_map/far_tiles/pallas_call | solution.py:249
  63.8 0.0 copy-done
  63.8 3.3 %collective-permute-start = (bf16[384,256]{1,0:T(8,128)(2,1)S(1)}, bf16[384,256]{1,0:T(8,128)(2,1)S(1)}, u32[]{:S(2)}, u32[]{:S(2)}) collective-permute-start(bf16[384,256]{1,0:T(8,128)(2,1)S(1)} %get-tuple-element.17), channel_id=1, source_target_pairs={{0,1},{1,2},{2,3},{3,4},{4,5},{5,6},{6,7},{7,8},{8,9},{9,10},{10,1... | collective-permute-start | bytes 589832 | tf_op jit(solution)/shard_map/ppermute | solution.py:263
  67.1 8.5 %collective-permute-start.1 = (bf16[384,256]{1,0:T(8,128)(2,1)S(1)}, bf16[384,256]{1,0:T(8,128)(2,1)S(1)}, u32[]{:S(2)}, u32[]{:S(2)}) collective-permute-start(bf16[384,256]{1,0:T(8,128)(2,1)S(1)} %get-tuple-element.18), channel_id=1, source_target_pairs={{1,0},{2,1},{3,2},{4,3},{5,4},{6,5},{7,6},{8,7},{9,8},{10,9},{11,1... | collective-permute-start | bytes 589832 | tf_op jit(solution)/shard_map/ppermute | solution.py:262
  75.7 14.8 %inner_tiles.1 = (f32[96,128,128]{2,1,0:T(8,128)}, f32[96,128,128]{2,1,0:T(8,128)}, bf16[512,1024]{1,0:T(8,128)(2,1)}, bf16[512,1024]{1,0:T(8,128)(2,1)}, bf16[4...) custom-call(s32[96]{0:T(128)} %select_reduce_fusion.keys_ref, s32[17]{0:T(128)} %convert_reduce_fusion.1.ends_ref, ...), custom_call_target="tpu_custom_call" | custom-call | flops 7851737088 | bytes 20971520 | tf_op jit(solution)/shard_map/inner_tiles/pallas_call | solution.py:266
  90.5 6.3 %collective-permute-done.far_l = bf16[384,256]{1,0:T(8,128)(2,1)S(1)} collective-permute-done((bf16[384,256]{1,0:T(8,128)(2,1)S(1)}, bf16[384,256]{1,0:T(8,128)(2,1)S(1)}, u32[]{:S(2)}, u32[]{:S(2)}) %collective-permute-start) | collective-permute-done | bytes 196640 | tf_op jit(solution)/shard_map/ppermute | solution.py:263
  96.8 0.0 copy-start.1
  96.8 0.0 collective-permute-done.1.far_r
  96.8 0.0 copy-start.2
  96.8 0.0 all-to-all-done.1
  96.8 0.7 copy-done.1
  97.5 0.1 copy-done.2
  97.5 11.0 %edge_tiles.1 = (f32[96,128,128]{2,1,0:T(8,128)}, f32[96,128,128]{2,1,0:T(8,128)}) custom-call(s32[96]{0:T(128)} %select_reduce_fusion.keys_ref, s32[17]{0:T(128)} %convert_reduce_fusion.1.ends_ref, bf16[384,256]{1,0:T(8,128)(2,1)} %copy-done.1, bf16[384,256]{1,0:T(8,128)(2,1)} %copy-done.2, ...), custom_call_target="tpu_custom_call", output_to_operand_aliasing={{0}: (9, {}), {1}: (10, {})} | custom-call | flops 3355443200 | bytes 16777216 | tf_op jit(solution)/shard_map/edge_tiles/pallas_call | solution.py:286
  (4 shorter events, 0.1 us)
Async XLA Ops:
  0.6 11.5 %copy-start.3 = (s32[96,2]{0,1:T(2,128)S(1)}, s32[96,2]{0,1:T(2,128)}, u32[]{:S(2)}) copy-start(s32[96,2]{0,1:T(2,128)} %param.3) | copy-start | bytes 2308
  0.6 55.3 %all-to-all-start = ((bf16[8,128,1664]{2,0,1:T(8,128)(2,1)}), bf16[8,128,1664]{2,0,1:T(8,128)(2,1)S(1)}, u32[]{:S(2)}, u32[]{:S(2)}) async-start(bf16[8,128,1664]{2,0,1:T(8,128)(2,1)} %bitcast.87), calls=%async_computation | async-start | bytes 6815744 | tf_op jit(solution)/shard_map/all_to_all | solution.py:233
  55.9 7.9 %copy-start = (bf16[8,128,1664]{2,0,1:T(8,128)(2,1)}, bf16[8,128,1664]{2,0,1:T(8,128)(2,1)S(1)}, u32[]{:S(2)}) copy-start(bf16[8,128,1664]{2,0,1:T(8,128)(2,1)S(1)} %all-to-all-done) | copy-start | bytes 10223620
  55.9 40.9 %all-to-all-start.1 = ((bf16[8,128,1024]{2,0,1:T(8,128)(2,1)}), bf16[8,128,1024]{2,0,1:T(8,128)(2,1)}, u32[]{:S(2)}, u32[]{:S(2)}) async-start(bf16[8,128,1024]{2,0,1:T(8,128)(2,1)} %fusion.2), calls=%async_computation.1 | async-start | bytes 4194304 | tf_op jit(solution)/shard_map/all_to_all | solution.py:245
  63.8 33.0 %collective-permute-start = (bf16[384,256]{1,0:T(8,128)(2,1)S(1)}, bf16[384,256]{1,0:T(8,128)(2,1)S(1)}, u32[]{:S(2)}, u32[]{:S(2)}) collective-permute-start(bf16[384,256]{1,0:T(8,128)(2,1)S(1)} %get-tuple-element.17), channel_id=1, source_target_pairs={{0,1},{1,2},{2,3},{3,4},{4,5},{5,6},{6,7},{7,8},{8,9},{9,10},{10,1... | collective-permute-start | bytes 589832 | tf_op jit(solution)/shard_map/ppermute | solution.py:263
  67.1 29.7 %collective-permute-start.1 = (bf16[384,256]{1,0:T(8,128)(2,1)S(1)}, bf16[384,256]{1,0:T(8,128)(2,1)S(1)}, u32[]{:S(2)}, u32[]{:S(2)}) collective-permute-start(bf16[384,256]{1,0:T(8,128)(2,1)S(1)} %get-tuple-element.18), channel_id=1, source_target_pairs={{1,0},{2,1},{3,2},{4,3},{5,4},{6,5},{7,6},{8,7},{9,8},{10,9},{11,1... | collective-permute-start | bytes 589832 | tf_op jit(solution)/shard_map/ppermute | solution.py:262
  96.8 0.7 copy-start.1
  96.8 0.7 copy-start.2

commit v3 on v2

v3 whole, which is shorter than its diff:
```python
import functools

import jax
import jax.numpy as jnp
from jax import lax
from jax.experimental import pallas as pl
from jax.experimental.pallas import tpu as pltpu
from jax.sharding import PartitionSpec as P

BS = 128
LAG = 16
BAND = 4
REACH = 2
HALO = 4
SPAN = 2 * BAND + 1
ROWS = REACH + BAND
COLS = HALO + BAND
SLOT = 128
AXES = ("frames", "feat")
F32 = jnp.float32
BF16 = jnp.bfloat16
VMEM = pl.BlockSpec(memory_space=pltpu.VMEM)
HBM = pl.BlockSpec(memory_space=pl.ANY)


def far_tiles(blocks):
    low, high = [], []
    for col in range(HALO, REACH + BAND):
        low.append((col, list(range(max(0, col - BAND), REACH))))
    for col in range(blocks - 1 - HALO, blocks - 1 - REACH - BAND, -1):
        high.append((col, list(range(blocks - REACH, min(blocks, col + BAND + 1)))))
    return low, high


def far_count():
    reach = REACH + BAND - HALO
    return reach * (reach + 1) // 2


def centred(panels_ref, b):
    panel = panels_ref[:, b * BS : (b + 1) * BS].astype(F32)
    mean = jnp.sum(panel, axis=0, keepdims=True) * (1.0 / panel.shape[0])
    return (panel - mean).astype(BF16)


def pair_into(pair_ref, slot, panel):
    frames = panel.shape[0]
    pair_ref[slot, :, :BS] = panel
    pair_ref[slot, : frames - LAG, BS:] = panel[LAG:]
    pair_ref[slot, frames - LAG :, BS:] = jnp.zeros((LAG, BS), BF16)


def block_rows(first, last):
    return slice(first * BS, last * BS)


def copies(key, res, out_i, out_l, sems, base):
    at = lax.shift_right_logical(key, 7) - base
    tile = lax.bitwise_and(key, SLOT - 1)
    return (
        pltpu.make_async_copy(res.at[at, 0], out_i.at[tile], sems.at[tile, 0]),
        pltpu.make_async_copy(res.at[at, 1], out_l.at[tile], sems.at[tile, 1]),
    )


def start_run(meta_ref, first, last, *where):
    @pl.loop(first, last)
    def _(r):
        for copy in copies(meta_ref[r], *where):
            copy.start()


def wait_run(meta_ref, first, last, *where):
    @pl.loop(first, last)
    def _(r):
        for copy in copies(meta_ref[r], *where):
            copy.wait()


def keep(res, at, part, frames):
    res[at, 0] = part[:, :BS] * (1.0 / (frames - 1))
    res[at, 1] = part[:, BS:] * (1.0 / (frames - LAG))


def inner_kernel(
    blocks, groups, tiles, meta_hbm, own_ref, out_i, out_l, edge_l, edge_r, low_ref, high_ref,
    meta_ref, turned, pair, res, far, sems, side_sems
):
    frames = own_ref.shape[0]
    where = (res, out_i, out_l, sems, 0)
    meta_copy = pltpu.make_async_copy(meta_hbm, meta_ref, side_sems.at[2])
    meta_copy.start()

    def ends(group):
        return meta_ref[tiles + group]

    side_copies = [
        pltpu.make_async_copy(pair.at[pl.ds(at, BAND), :, pl.ds(0, BS)], ref, side_sems.at[side])
        for side, (at, ref) in enumerate(((0, edge_l), (blocks - BAND, edge_r)))
    ]
    far_places = [[(row, col) for col, rows in side for row in rows] for side in far_tiles(blocks)]
    ready = 0
    first = 0
    for end in groups:
        for b in range(ready, min(blocks, end + BAND)):
            panel = centred(own_ref, b)
            turned[block_rows(b, b + 1), :] = panel.T
            pair_into(pair, b, panel)
        if ready < blocks <= end + BAND:
            for copy in side_copies:
                copy.start()
        ready = min(blocks, end + BAND)
        for col in range(first, end):
            low, high = max(0, col - BAND), min(blocks, col + BAND + 1)
            prod = jnp.dot(turned[block_rows(low, high), :], pair[col], preferred_element_type=F32)
            for row in range(low, high):
                at = col * SPAN + row - col + BAND
                keep(res, at, prod[block_rows(row - low, row - low + 1)], frames)
                for side, tiles_far in enumerate(far_places):
                    if (row, col) in tiles_far:
                        t = tiles_far.index((row, col))
                        for half in range(2):
                            far[side, block_rows(t, t + 1), half * BS : (half + 1) * BS] = res[at, half].astype(BF16)
        if first == 0:
            meta_copy.wait()
        start_run(meta_ref, ends(first), ends(end), *where)
        first = end
    far_copies = [
        pltpu.make_async_copy(far.at[side], ref, side_sems.at[3 + side]) for side, ref in enumerate((low_ref, high_ref))
    ]
    for copy in far_copies:
        copy.start()
    for copy in side_copies + far_copies:
        copy.wait()
    wait_run(meta_ref, 0, ends(blocks), *where)


def edge_kernel(
    blocks, base, tiles, meta_hbm, edge_l, edge_r, halo_ref, in_i, in_l,
    out_i, out_l, meta_ref, own, turned, pair, res, sems, in_sems,
):
    del in_i, in_l
    frames = halo_ref.shape[0]
    where = (res, out_i, out_l, sems, base)
    halo0, own0, row0 = (0, BAND), (HALO, 0), (HALO - REACH, 0)

    def copy_in(src, dst, at):
        copy = pltpu.make_async_copy(src, dst, in_sems.at[at])
        copy.start()
        return copy

    own_copies = []
    for side, edge_ref in enumerate((edge_l, edge_r)):
        own_copies.append(copy_in(edge_ref, own.at[side], side))
    meta_copy = pltpu.make_async_copy(meta_hbm, meta_ref, in_sems.at[2])
    meta_copy.start()

    def ends(group):
        return meta_ref[tiles + group]

    for side in range(2):

        def place(col, panel):
            pair_into(pair.at[side], col, panel)
            row = col - row0[side]
            if 0 <= row < ROWS:
                turned[side, block_rows(row, row + 1), :] = panel.T

        for b in range(HALO):
            place(halo0[side] + b, centred(halo_ref, side * HALO + b))
        own_copies[side].wait()
        for b in range(BAND):
            place(own0[side] + b, own[side, b])
        for col in range(COLS):
            rows = [row for row in range(ROWS) if abs(row + row0[side] - col) <= BAND]
            if own0[side] <= col < own0[side] + BAND:
                rows = [row for row in rows if (row < REACH if side == 0 else row >= BAND)]
            low, high = rows[0], rows[-1] + 1
            prod = jnp.dot(turned[side, block_rows(low, high), :], pair[side, col], preferred_element_type=F32)
            for row in rows:
                at = (side * ROWS + row) * COLS + col
                keep(res, at, prod[block_rows(row - low, row - low + 1)], frames)
        if side == 0:
            meta_copy.wait()
        start_run(meta_ref, ends(blocks + 1 + side), ends(blocks + 2 + side), *where)
    wait_run(meta_ref, ends(blocks + 1), tiles, *where)


def last_kernel(blocks, base, tiles, meta_hbm, far_l, far_r, in_i, in_l, out_i, out_l, meta_ref, res, sems, meta_sem):
    del in_i, in_l
    where = (res, out_i, out_l, sems, base)
    meta_copy = pltpu.make_async_copy(meta_hbm, meta_ref, meta_sem)
    meta_copy.start()
    count = far_count()
    for other, far in enumerate((far_l, far_r)):
        for t in range(count):
            for half in range(2):
                res[other * count + t, half] = far[block_rows(t, t + 1), half * BS : (half + 1) * BS].astype(F32)
    meta_copy.wait()
    first, last = meta_ref[tiles + blocks], meta_ref[tiles + blocks + 1]
    start_run(meta_ref, first, last, *where)
    wait_run(meta_ref, first, last, *where)


def sorted_keys(tile_list, blocks):
    tiles = tile_list.shape[0]
    rel = tile_list - lax.axis_index(AXES) * blocks
    row, col = rel[:, 0], rel[:, 1]
    inner = col * SPAN + row - col + BAND
    far0 = blocks * SPAN
    reach = REACH + BAND - HALO
    below = -HALO - 1 - col
    above = col - (blocks + HALO)

    def before(step):
        return step * reach - step * (step - 1) // 2

    far_low = far0 + before(below) + row + REACH
    far_high = far0 + far_count() + before(above) + row - (blocks + HALO - BAND) - above
    left0 = far0 + 2 * far_count()
    right0 = left0 + ROWS * COLS
    left = left0 + (row + REACH) * COLS + col + HALO
    right = right0 + (row - (blocks - BAND)) * COLS + col - (blocks - BAND)
    place = jnp.where((row >= blocks) | (col >= blocks), right, inner)
    place = jnp.where((row < 0) | (col < 0), left, place)
    place = jnp.where(below >= 0, far_low, jnp.where(above >= 0, far_high, place))
    key = place * SLOT + lax.iota(jnp.int32, tiles)
    rank = jnp.sum((key[None, :] < key[:, None]).astype(jnp.int32), axis=1)
    keys = jnp.sum(jnp.where(rank[None, :] == lax.iota(jnp.int32, tiles)[:, None], key[None, :], 0), axis=1)
    number = lax.iota(jnp.int32, blocks + 4)
    edges = number * SPAN
    for at, value in ((1, left0), (2, right0), (3, right0 + ROWS * COLS)):
        edges = jnp.where(number == blocks + at, value, edges)
    ends = jnp.sum((key[None, :] < edges[:, None] * SLOT).astype(jnp.int32), axis=1)
    return jnp.concatenate([keys, ends, jnp.zeros((-(tiles + blocks + 4) % SLOT,), jnp.int32)]), far0


def per_device(trajectory, tile_list):
    count = lax.axis_size(AXES)
    parts = trajectory.reshape(trajectory.shape[0], count, -1)
    blocks = parts.shape[2] // BS
    tiles = tile_list.shape[0]
    own = lax.all_to_all(trajectory, AXES, split_axis=1, concat_axis=0, tiled=True)
    frames = own.shape[0]
    edge = HALO * BS
    beside = jnp.concatenate(
        [
            jnp.pad(parts[:, :-1, parts.shape[2] - edge :], ((0, 0), (1, 0), (0, 0))),
            jnp.pad(parts[:, 1:, :edge], ((0, 0), (0, 1), (0, 0))),
        ],
        axis=2,
    )
    meta, base = sorted_keys(tile_list, blocks)
    own, beside, meta = lax.optimization_barrier((own, beside, meta))
    words = pltpu.SMEM(meta.shape, jnp.int32)
    halo = lax.all_to_all(beside, AXES, split_axis=1, concat_axis=0, tiled=True).reshape(frames, 2 * edge)

    far = far_count()
    outs = [jax.ShapeDtypeStruct((tiles, BS, BS), F32)] * 2
    inst, lagg, edge_l, edge_r, to_left, to_right = pl.pallas_call(
        functools.partial(inner_kernel, blocks, (blocks,), tiles),
        out_shape=outs + [jax.ShapeDtypeStruct((BAND, frames, BS), BF16)] * 2
        + [jax.ShapeDtypeStruct((far * BS, 2 * BS), BF16)] * 2,
        in_specs=[HBM, VMEM],
        out_specs=[HBM] * 6,
        scratch_shapes=[
            words,
            pltpu.VMEM((blocks * BS, frames), BF16),
            pltpu.VMEM((blocks, frames, 2 * BS), BF16),
            pltpu.VMEM((blocks * SPAN, 2, BS, BS), F32),
            pltpu.VMEM((2, far * BS, 2 * BS), BF16),
            pltpu.SemaphoreType.DMA((tiles, 2)),
            pltpu.SemaphoreType.DMA((5,)),
        ],
        compiler_params=pltpu.CompilerParams(vmem_limit_bytes=52 << 20),
        cost_estimate=pl.CostEstimate(
            flops=blocks * SPAN * 4 * BS * BS * frames, bytes_accessed=20 << 20, transcendentals=0
        ),
        name="inner_tiles",
    )(meta, own)
    far_r = lax.ppermute(to_left, AXES, [(i + 1, i) for i in range(count - 1)])
    far_l = lax.ppermute(to_right, AXES, [(i, i + 1) for i in range(count - 1)])
    inst, lagg = pl.pallas_call(
        functools.partial(edge_kernel, blocks, base + 2 * far, tiles),
        out_shape=outs,
        in_specs=[HBM, HBM, HBM, VMEM, HBM, HBM],
        out_specs=[HBM, HBM],
        scratch_shapes=[
            words,
            pltpu.VMEM((2, BAND, frames, BS), BF16),
            pltpu.VMEM((2, ROWS * BS, frames), BF16),
            pltpu.VMEM((2, COLS, frames, 2 * BS), BF16),
            pltpu.VMEM((2 * ROWS * COLS, 2, BS, BS), F32),
            pltpu.SemaphoreType.DMA((tiles, 2)),
            pltpu.SemaphoreType.DMA((3,)),
        ],
        input_output_aliases={4: 0, 5: 1},
        compiler_params=pltpu.CompilerParams(vmem_limit_bytes=36 << 20),
        cost_estimate=pl.CostEstimate(flops=50 * 4 * BS * BS * frames, bytes_accessed=16 << 20, transcendentals=0),
        name="edge_tiles",
    )(meta, edge_l, edge_r, halo, inst, lagg)
    inst, lagg = pl.pallas_call(
        functools.partial(last_kernel, blocks, base, tiles),
        out_shape=outs,
        in_specs=[HBM, VMEM, VMEM, HBM, HBM],
        out_specs=[HBM, HBM],
        scratch_shapes=[
            words,
            pltpu.VMEM((2 * far, 2, BS, BS), F32),
            pltpu.SemaphoreType.DMA((tiles, 2)),
            pltpu.SemaphoreType.DMA,
        ],
        input_output_aliases={3: 0, 4: 1},
        compiler_params=pltpu.CompilerParams(vmem_limit_bytes=16 << 20),
        name="last_tiles",
    )(meta, far_l, far_r, inst, lagg)
    return (inst, lagg)


def solution(mesh):
    in_specs = (P(AXES, None), P(AXES, None))
    out_specs = (P(AXES, None, None), P(AXES, None, None))
    return jax.shard_map(per_device, mesh=mesh, in_specs=in_specs, out_specs=out_specs, check_vma=False)
```

time: 109 us -> 105 us (0.963)
  waiting for transfers between devices: 45.2 us -> 42.2 us
  Pallas kernels: 27.1 us -> 28.4 us
    ppermute x1, waiting for transfers between devices: 6.3 us -> 0.01 us  [per_device(): far_l = lax.ppermute(to_right, AXES, [(i, i + 1) for i in range(count - 1)])]
    all_to_all x1, waiting for transfers between devices: 38.9 us -> 41 us  [per_device(): lax.all_to_all(trajectory, AXES, split_axis=1, concat_axis=0, tiled=True)]
    slice x1, local copies, waits for them, and re-layouts: 1.68 us -> 0.16 us  [per_device(): parts[:, :-1, parts.shape[2] - edge:]]
    pallas_call x3, Pallas kernels: 27.1 us -> 28.4 us  [the longest x1 16.8 us: per_device(): pl.pallas_call(functools.partial(inner_kernel, blocks, (blocks,), tiles),...]
    all_to_all x1, waiting for transfers between devices: 0.01 us -> 1.22 us  [per_device(): lax.all_to_all(beside, AXES, split_axis=1, concat_axis=0, tiled=True)]
  transfers between devices with their start and end apart: 4 -> 4, of which waited for: 2 -> 2; matrix products, arithmetic and copies ran while one was open for 4% -> 2% of each run, Pallas kernels for 15% -> 24%
where the time goes in v3:
time: 105 us
  waiting for transfers between devices  42.2 us (40%)
  starting transfers between devices  29.4 us (28%)
  Pallas kernels  28.4 us (27%)
  other arithmetic  2.22 us (2%)
  local copies, waits for them, and re-layouts  1.39 us (1%)
    all_to_all x1, waiting for transfers between devices, per_device(): lax.all_to_all(trajectory, AXES, split_axis=1, concat_axis=0, tiled=True)  41 us
    pallas_call x1, Pallas kernels, per_device(): pl.pallas_call(functools.partial(inner_kernel, blocks, (blocks,), tiles),...  16.8 us
    all_to_all x1, starting transfers between devices, per_device(): lax.all_to_all(trajectory, AXES, split_axis=1, concat_axis=0, tiled=True)  11.9 us
    pallas_call x1, Pallas kernels, per_device(): pl.pallas_call(functools.partial(edge_kernel, blocks, base + 2 * far, til...  8.44 us
    ppermute x1, starting transfers between devices, per_device(): far_r = lax.ppermute(to_left, AXES, [(i + 1, i) for i in range(count - 1)])  8.4 us
    all_to_all x1, starting transfers between devices, per_device(): lax.all_to_all(beside, AXES, split_axis=1, concat_axis=0, tiled=True)  6.18 us
    pallas_call x1, Pallas kernels, per_device(): pl.pallas_call(functools.partial(last_kernel, blocks, base, tiles), out_s...  3.19 us
    ppermute x1, starting transfers between devices, per_device(): far_l = lax.ppermute(to_right, AXES, [(i, i + 1) for i in range(count - 1)])  2.89 us
  transfers between devices with their start and end apart: 4, of which 2 were waited for; matrix products, arithmetic and copies ran while one was open for 2% of the time, Pallas kernels for 24%

profile of v3, /device:TPU:1, one launch (start us, length us, event | category | flops | bytes accessed | tf_op | source)
XLA Modules:
  0.0 104.6 jit_solution(8212272037148933970)
XLA Ops:
  0.6 0.0 copy-start.1
  0.6 0.0 copy-start.2
  0.6 11.9 %all-to-all-start = ((bf16[8,128,1664]{2,0,1:T(8,128)(2,1)}), bf16[8,128,1664]{2,0,1:T(8,128)(2,1)}, u32[]{:S(2)}, u32[]{:S(2)}) async-start(bf16[8,128,1664]{2,0,1:T(8,128)(2,1)} %bitcast.86), calls=%async_computation | async-start | bytes 6815744 | tf_op jit(solution)/shard_map/all_to_all | solution.py:243
  12.6 0.0 copy-done.2
  12.7 0.2 convert_reduce_fusion
  12.8 0.1 select_reduce_fusion
  13.0 0.2 convert_reduce_fusion.1
  13.1 0.1 pad_add_fusion.meta_hbm
  13.2 0.0 copy-done.1
  13.2 0.2 fusion.24
  13.4 1.6 %fusion.2 = bf16[8,128,1024]{2,0,1:T(8,128)(2,1)} fusion(bf16[8,127,512]{2,0,1:T(8,128)(2,1)S(1)} %get-tuple-element.25, bf16[8,127,512]{2,0,1:T(8,128)(2,1)S(1)} %get-tuple-element.24), kind=kLoop, calls=%fused_computation.4 | loop fusion | flops 8388608 | bytes 4177920 | tf_op jit(solution)/shard_map/concatenate | solution.py:246
  15.0 41.0 %all-to-all-done = bf16[8,128,1664]{2,0,1:T(8,128)(2,1)} async-done(((bf16[8,128,1664]{2,0,1:T(8,128)(2,1)}), bf16[8,128,1664]{2,0,1:T(8,128)(2,1)}, u32[]{:S(2)}, u32[]{:S(2)}) %all-to-all-start) | async-done | bytes 3407904 | tf_op jit(solution)/shard_map/all_to_all | solution.py:243
  56.0 6.2 %all-to-all-start.1 = ((bf16[8,128,1024]{2,0,1:T(8,128)(2,1)}), bf16[8,128,1024]{2,0,1:T(8,128)(2,1)S(1)}, u32[]{:S(2)}, u32[]{:S(2)}) async-start(bf16[8,128,1024]{2,0,1:T(8,128)(2,1)} %fusion.2), calls=%async_computation.1 | async-start | bytes 4194304 | tf_op jit(solution)/shard_map/all_to_all | solution.py:256
  62.2 16.8 %inner_tiles.1 = (f32[96,128,128]{2,1,0:T(8,128)}, f32[96,128,128]{2,1,0:T(8,128)}, bf16[4,1024,128]{2,1,0:T(8,128)(2,1)S(1)}, bf16[4,1024,128]{2,1,0:T(8,128)(2...) custom-call(s32[128]{0:T(128)S(1)} %pad_add_fusion.meta_hbm, bf16[1024,1664]{1,0:T(8,128)(2,1)} %bitcast.2.own_ref), custom_call_target="tpu_custom_call" | custom-call | flops 7851737088 | bytes 20971520 | tf_op jit(solution)/shard_map/inner_tiles/pallas_call | solution.py:260
  79.0 2.9 %collective-permute-start = (bf16[384,256]{1,0:T(8,128)(2,1)}, bf16[384,256]{1,0:T(8,128)(2,1)S(1)}, u32[]{:S(2)}, u32[]{:S(2)}) collective-permute-start(bf16[384,256]{1,0:T(8,128)(2,1)} %get-tuple-element.15), channel_id=1, source_target_pairs={{0,1},{1,2},{2,3},{3,4},{4,5},{5,6},{6,7},{7,8},{8,9},{9,10},{10,1... | collective-permute-start | bytes 589832 | tf_op jit(solution)/shard_map/ppermute | solution.py:282
  81.9 8.4 %collective-permute-start.1 = (bf16[384,256]{1,0:T(8,128)(2,1)}, bf16[384,256]{1,0:T(8,128)(2,1)S(1)}, u32[]{:S(2)}, u32[]{:S(2)}) collective-permute-start(bf16[384,256]{1,0:T(8,128)(2,1)} %get-tuple-element.16), channel_id=1, source_target_pairs={{1,0},{2,1},{3,2},{4,3},{5,4},{6,5},{7,6},{8,7},{9,8},{10,9},{11,1... | collective-permute-start | bytes 589832 | tf_op jit(solution)/shard_map/ppermute | solution.py:281
  90.3 1.2 %all-to-all-done.1 = bf16[8,128,1024]{2,0,1:T(8,128)(2,1)S(1)} async-done(((bf16[8,128,1024]{2,0,1:T(8,128)(2,1)}), bf16[8,128,1024]{2,0,1:T(8,128)(2,1)S(1)}, u32[]{:S(2)}, u32[]{:S(2)}) %all-to-all-start.1) | async-done | bytes 2097184 | tf_op jit(solution)/shard_map/all_to_all | solution.py:256
  91.5 0.0 copy-start
  91.5 1.2 %copy-done = bf16[4,1024,128]{2,1,0:T(8,128)(2,1)S(1)} copy-done((bf16[4,1024,128]{2,1,0:T(8,128)(2,1)S(1)}, bf16[4,1024,128]{2,1,0:T(8,128)(2,1)}, u32[]{:S(2)}) %copy-start) | copy-done | bytes 1048600
  92.7 8.4 %edge_tiles.1 = (f32[96,128,128]{2,1,0:T(8,128)}, f32[96,128,128]{2,1,0:T(8,128)}) custom-call(s32[128]{0:T(128)S(1)} %pad_add_fusion.meta_hbm, bf16[4,1024,128]{2,1,0:T(8,128)(2,1)S(1)} %get-tuple-element.17.edge_l, bf16[4,1024,128]{2,1,0:T(8,128)(2,1)S(1)} %copy-done, ...), custom_call_target="tpu_custom_call", output_to_operand_aliasing={{0}: (4, {}), {1}: (5, {})} | custom-call | flops 3355443200 | bytes 16777216 | tf_op jit(solution)/shard_map/edge_tiles/pallas_call | solution.py:283
  101.2 0.0 collective-permute-done.far_l
  101.2 0.0 collective-permute-done.1.far_r
  101.2 3.2 %last_tiles.1 = (f32[96,128,128]{2,1,0:T(8,128)}, f32[96,128,128]{2,1,0:T(8,128)}) custom-call(s32[128]{0:T(128)S(1)} %pad_add_fusion.meta_hbm, bf16[384,256]{1,0:T(8,128)(2,1)S(1)} %collective-permute-done.far_l, bf16[384,256]{1,0:T(8,128)(2,1)S(1)} %collective-permute-done.1.far_r, ...), custom_call_target="tpu_custom_call", output_to_operand_aliasing={{0}: (3, {}), {1}: (4, {})} | custom-call | tf_op jit(solution)/shard_map/last_tiles/pallas_call | solution.py:302
  (5 shorter events, 0.1 us)
Async XLA Ops:
  0.6 12.6 %copy-start.1 = (bf16[8,212992]{1,0:T(8,128)(2,1)S(1)}, bf16[8,212992]{1,0:T(8,128)(2,1)}, u32[]{:S(2)}) copy-start(bf16[8,212992]{1,0:T(8,128)(2,1)} %param.2) | copy-start | bytes 10223620
  0.6 11.9 %copy-start.2 = (s32[96,2]{0,1:T(2,128)S(1)}, s32[96,2]{0,1:T(2,128)}, u32[]{:S(2)}) copy-start(s32[96,2]{0,1:T(2,128)} %param.3) | copy-start | bytes 2308
  0.6 55.4 %all-to-all-start = ((bf16[8,128,1664]{2,0,1:T(8,128)(2,1)}), bf16[8,128,1664]{2,0,1:T(8,128)(2,1)}, u32[]{:S(2)}, u32[]{:S(2)}) async-start(bf16[8,128,1664]{2,0,1:T(8,128)(2,1)} %bitcast.86), calls=%async_computation | async-start | bytes 6815744 | tf_op jit(solution)/shard_map/all_to_all | solution.py:243
  56.0 35.5 %all-to-all-start.1 = ((bf16[8,128,1024]{2,0,1:T(8,128)(2,1)}), bf16[8,128,1024]{2,0,1:T(8,128)(2,1)S(1)}, u32[]{:S(2)}, u32[]{:S(2)}) async-start(bf16[8,128,1024]{2,0,1:T(8,128)(2,1)} %fusion.2), calls=%async_computation.1 | async-start | bytes 4194304 | tf_op jit(solution)/shard_map/all_to_all | solution.py:256
  79.0 22.2 %collective-permute-start = (bf16[384,256]{1,0:T(8,128)(2,1)}, bf16[384,256]{1,0:T(8,128)(2,1)S(1)}, u32[]{:S(2)}, u32[]{:S(2)}) collective-permute-start(bf16[384,256]{1,0:T(8,128)(2,1)} %get-tuple-element.15), channel_id=1, source_target_pairs={{0,1},{1,2},{2,3},{3,4},{4,5},{5,6},{6,7},{7,8},{8,9},{9,10},{10,1... | collective-permute-start | bytes 589832 | tf_op jit(solution)/shard_map/ppermute | solution.py:282
  81.9 19.3 %collective-permute-start.1 = (bf16[384,256]{1,0:T(8,128)(2,1)}, bf16[384,256]{1,0:T(8,128)(2,1)S(1)}, u32[]{:S(2)}, u32[]{:S(2)}) collective-permute-start(bf16[384,256]{1,0:T(8,128)(2,1)} %get-tuple-element.16), channel_id=1, source_target_pairs={{1,0},{2,1},{3,2},{4,3},{5,4},{6,5},{7,6},{8,7},{9,8},{10,9},{11,1... | collective-permute-start | bytes 589832 | tf_op jit(solution)/shard_map/ppermute | solution.py:281
  91.5 1.2 %copy-start = (bf16[4,1024,128]{2,1,0:T(8,128)(2,1)S(1)}, bf16[4,1024,128]{2,1,0:T(8,128)(2,1)}, u32[]{:S(2)}) copy-start(bf16[4,1024,128]{2,1,0:T(8,128)(2,1)} %get-tuple-element.18.edge_r) | copy-start | bytes 3145732

commit v4 on v3

v4 whole, which is shorter than its diff:
```python
import functools

import jax
import jax.numpy as jnp
from jax import lax
from jax.experimental import pallas as pl
from jax.experimental.pallas import tpu as pltpu
from jax.sharding import PartitionSpec as P

BS = 128
LAG = 16
BAND = 4
REACH = 2
HALO = 4
SPAN = 2 * BAND + 1
ROWS = REACH + BAND
COLS = HALO + BAND
KEPT = 16
SLOT = 128
AXES = ("frames", "feat")
F32 = jnp.float32
BF16 = jnp.bfloat16
VMEM = pl.BlockSpec(memory_space=pltpu.VMEM)
HBM = pl.BlockSpec(memory_space=pl.ANY)


def far_tiles(blocks):
    low, high = [], []
    for col in range(HALO, REACH + BAND):
        low.append((col, list(range(max(0, col - BAND), REACH))))
    for col in range(blocks - 1 - HALO, blocks - 1 - REACH - BAND, -1):
        high.append((col, list(range(blocks - REACH, min(blocks, col + BAND + 1)))))
    return low, high


def far_count():
    reach = REACH + BAND - HALO
    return reach * (reach + 1) // 2


def centred(panels_ref, b):
    panel = panels_ref[:, b * BS : (b + 1) * BS].astype(F32)
    mean = jnp.sum(panel, axis=0, keepdims=True) * (1.0 / panel.shape[0])
    return (panel - mean).astype(BF16)


def pair_into(pair_ref, slot, panel):
    frames = panel.shape[0]
    pair_ref[slot, :, :BS] = panel
    pair_ref[slot, : frames - LAG, BS:] = panel[LAG:]
    pair_ref[slot, frames - LAG :, BS:] = jnp.zeros((LAG, BS), BF16)


def block_rows(first, last):
    return slice(first * BS, last * BS)


def copies(key, res, out_i, out_l, sems, base):
    at = lax.shift_right_logical(key, 7) - base
    tile = lax.bitwise_and(key, SLOT - 1)
    return (
        pltpu.make_async_copy(res.at[at, 0], out_i.at[tile], sems.at[tile, 0]),
        pltpu.make_async_copy(res.at[at, 1], out_l.at[tile], sems.at[tile, 1]),
    )


def start_run(meta_ref, first, last, *where):
    @pl.loop(first, last)
    def _(r):
        for copy in copies(meta_ref[r], *where):
            copy.start()


def wait_run(meta_ref, first, last, *where):
    @pl.loop(first, last)
    def _(r):
        for copy in copies(meta_ref[r], *where):
            copy.wait()


def keep(res, at, part, frames):
    res[at, 0] = part[:, :BS] * (1.0 / (frames - 1))
    res[at, 1] = part[:, BS:] * (1.0 / (frames - LAG))


def inner_kernel(
    blocks, groups, tiles, meta_hbm, own_ref, out_i, out_l, edge_ref, low_ref, high_ref,
    meta_ref, turned, pair, res, far, sems, side_sems
):
    frames = own_ref.shape[0]
    where = (res, out_i, out_l, sems, 0)
    meta_copy = pltpu.make_async_copy(meta_hbm, meta_ref, side_sems.at[2])
    meta_copy.start()

    def ends(group):
        return meta_ref[tiles + group]

    side_copies = [
        pltpu.make_async_copy(pair.at[pl.ds(at, BAND), :, pl.ds(0, BS)], edge_ref.at[side], side_sems.at[side])
        for side, at in enumerate((0, blocks - BAND))
    ]
    far_places = [[(row, col) for col, rows in side for row in rows] for side in far_tiles(blocks)]
    ready = 0
    first = 0
    for end in groups:
        for b in range(ready, min(blocks, end + BAND)):
            panel = centred(own_ref, b)
            turned[block_rows(b, b + 1), :] = panel.T
            pair_into(pair, b, panel)
        if ready < blocks <= end + BAND:
            for copy in side_copies:
                copy.start()
        ready = min(blocks, end + BAND)
        for col in range(first, end):
            low, high = max(0, col - BAND), min(blocks, col + BAND + 1)
            prod = jnp.dot(turned[block_rows(low, high), :], pair[col], preferred_element_type=F32)
            for row in range(low, high):
                at = col * SPAN + row - col + BAND
                keep(res, at, prod[block_rows(row - low, row - low + 1)], frames)
                for side, tiles_far in enumerate(far_places):
                    if (row, col) in tiles_far:
                        t = tiles_far.index((row, col))
                        for half in range(2):
                            far[side, block_rows(t, t + 1), half * BS : (half + 1) * BS] = res[at, half].astype(BF16)
        if first == 0:
            meta_copy.wait()
        start_run(meta_ref, ends(first), ends(end), *where)
        first = end
    far_copies = [
        pltpu.make_async_copy(far.at[side], ref, side_sems.at[3 + side]) for side, ref in enumerate((low_ref, high_ref))
    ]
    for copy in far_copies:
        copy.start()
    for copy in side_copies + far_copies:
        copy.wait()
    wait_run(meta_ref, 0, ends(blocks), *where)


def edge_kernel(blocks, side, base, tiles, meta_hbm, edge_ref, halo_ref, *refs):
    far_refs = refs[: 2 * side]
    out_i, out_l, meta_ref, own, turned, pair, res, sems, in_sems = refs[2 * side + 2 :]
    frames = halo_ref.shape[0]
    where = (res, out_i, out_l, sems, base)
    count = far_count() * len(far_refs)
    first_row = -REACH if side == 0 else blocks - BAND

    def block_of(slot):
        if slot < HALO:
            return slot - HALO if side == 0 else blocks + slot
        return slot - HALO + (0 if side == 0 else blocks - BAND)

    own_copy = pltpu.make_async_copy(edge_ref.at[side], own, in_sems.at[0])
    meta_copy = pltpu.make_async_copy(meta_hbm, meta_ref, in_sems.at[1])
    own_copy.start()
    meta_copy.start()

    def ends(group):
        return meta_ref[tiles + group]

    def place(slot):
        panel = centred(halo_ref, side * HALO + slot) if slot < HALO else own[slot - HALO]
        pair_into(pair, slot, panel)
        row = block_of(slot) - first_row
        if 0 <= row < ROWS:
            turned[block_rows(row, row + 1), :] = panel.T

    for other, far in enumerate(far_refs):
        for t in range(far_count()):
            for half in range(2):
                part = far[block_rows(t, t + 1), half * BS : (half + 1) * BS]
                res[other * far_count() + t, half] = part.astype(F32)
    for slot in range(HALO):
        place(slot)
    meta_copy.wait()
    if far_refs:
        start_run(meta_ref, ends(blocks + 2), ends(blocks + 3), *where)
    own_copy.wait()
    for slot in range(HALO, COLS):
        place(slot)
    group = blocks + 3 * side
    for slot in range(COLS):
        col = block_of(slot)
        rows = [row for row in range(ROWS) if abs(row + first_row - col) <= BAND]
        if slot >= HALO:
            rows = [row for row in rows if not 0 <= row + first_row < blocks]
        low, high = rows[0], rows[-1] + 1
        prod = jnp.dot(turned[block_rows(low, high), :], pair[slot], preferred_element_type=F32)
        for row in rows:
            keep(res, count + slot * ROWS + row, prod[block_rows(row - low, row - low + 1)], frames)
        if slot in (HALO - 1, COLS - 1):
            start_run(meta_ref, ends(group), ends(group + 1), *where)
            group += 1
    wait_run(meta_ref, ends(blocks + 2 * side), ends(blocks + 2 + 3 * side), *where)


def sorted_keys(tile_list, blocks):
    tiles = tile_list.shape[0]
    rel = tile_list - lax.axis_index(AXES) * blocks
    row, col = rel[:, 0], rel[:, 1]
    inner = col * SPAN + row - col + BAND
    reach = REACH + BAND - HALO
    below = -HALO - 1 - col
    above = col - (blocks + HALO)

    def before(step):
        return step * reach - step * (step - 1) // 2

    left0 = blocks * SPAN
    far0 = left0 + ROWS * COLS
    right0 = far0 + 2 * far_count()
    far_low = far0 + before(below) + row + REACH
    far_high = far0 + far_count() + before(above) + row - (blocks + HALO - BAND) - above
    left = left0 + (col + HALO) * ROWS + row + REACH
    slot = jnp.where(col >= blocks, col - blocks, col - (blocks - BAND) + HALO)
    right = right0 + slot * ROWS + row - (blocks - BAND)
    place = jnp.where((row >= blocks) | (col >= blocks), right, inner)
    place = jnp.where((row < 0) | (col < 0), left, place)
    place = jnp.where(below >= 0, far_low, jnp.where(above >= 0, far_high, place))
    key = place * SLOT + lax.iota(jnp.int32, tiles)
    rank = jnp.sum((key[None, :] < key[:, None]).astype(jnp.int32), axis=1)
    keys = jnp.sum(jnp.where(rank[None, :] == lax.iota(jnp.int32, tiles)[:, None], key[None, :], 0), axis=1)
    number = lax.iota(jnp.int32, blocks + 6)
    edges = number * SPAN
    starts = (left0 + HALO * ROWS, far0, right0, right0 + HALO * ROWS, right0 + COLS * ROWS)
    for at, value in enumerate(starts):
        edges = jnp.where(number == blocks + 1 + at, value, edges)
    ends = jnp.sum((key[None, :] < edges[:, None] * SLOT).astype(jnp.int32), axis=1)
    return jnp.concatenate([keys, ends, jnp.zeros((-(tiles + blocks + 6) % SLOT,), jnp.int32)]), (left0, far0)


def per_device(trajectory, tile_list):
    count = lax.axis_size(AXES)
    parts = trajectory.reshape(trajectory.shape[0], count, -1)
    blocks = parts.shape[2] // BS
    tiles = tile_list.shape[0]
    own = lax.all_to_all(trajectory, AXES, split_axis=1, concat_axis=0, tiled=True)
    frames = own.shape[0]
    edge = HALO * BS
    beside = jnp.concatenate(
        [
            jnp.pad(parts[:, :-1, parts.shape[2] - edge :], ((0, 0), (1, 0), (0, 0))),
            jnp.pad(parts[:, 1:, :edge], ((0, 0), (0, 1), (0, 0))),
        ],
        axis=2,
    )
    meta, bases = sorted_keys(tile_list, blocks)
    own, beside, meta = lax.optimization_barrier((own, beside, meta))
    words = pltpu.SMEM(meta.shape, jnp.int32)
    halo = lax.all_to_all(beside, AXES, split_axis=1, concat_axis=0, tiled=True).reshape(frames, 2 * edge)

    far = far_count()
    outs = [jax.ShapeDtypeStruct((tiles, BS, BS), F32)] * 2
    inst, lagg, edges, to_left, to_right = pl.pallas_call(
        functools.partial(inner_kernel, blocks, (blocks,), tiles),
        out_shape=outs + [jax.ShapeDtypeStruct((KEPT, BAND, frames, BS), BF16)]
        + [jax.ShapeDtypeStruct((far * BS, 2 * BS), BF16)] * 2,
        in_specs=[HBM, VMEM],
        out_specs=[HBM] * 5,
        scratch_shapes=[
            words,
            pltpu.VMEM((blocks * BS, frames), BF16),
            pltpu.VMEM((blocks, frames, 2 * BS), BF16),
            pltpu.VMEM((blocks * SPAN, 2, BS, BS), F32),
            pltpu.VMEM((2, far * BS, 2 * BS), BF16),
            pltpu.SemaphoreType.DMA((tiles, 2)),
            pltpu.SemaphoreType.DMA((5,)),
        ],
        compiler_params=pltpu.CompilerParams(vmem_limit_bytes=52 << 20),
        cost_estimate=pl.CostEstimate(
            flops=blocks * SPAN * 4 * BS * BS * frames, bytes_accessed=20 << 20, transcendentals=0
        ),
        name="inner_tiles",
    )(meta, own)
    far_r = lax.ppermute(to_left, AXES, [(i + 1, i) for i in range(count - 1)])
    far_l = lax.ppermute(to_right, AXES, [(i, i + 1) for i in range(count - 1)])
    for side, received in enumerate(((), (far_l, far_r))):
        far_tiles_in = far * len(received)
        inst, lagg = pl.pallas_call(
            functools.partial(edge_kernel, blocks, side, bases[side], tiles),
            out_shape=outs,
            in_specs=[HBM, HBM, VMEM] + [VMEM] * len(received) + [HBM, HBM],
            out_specs=[HBM, HBM],
            scratch_shapes=[
                words,
                pltpu.VMEM((BAND, frames, BS), BF16),
                pltpu.VMEM((ROWS * BS, frames), BF16),
                pltpu.VMEM((COLS, frames, 2 * BS), BF16),
                pltpu.VMEM((far_tiles_in + COLS * ROWS, 2, BS, BS), F32),
                pltpu.SemaphoreType.DMA((tiles, 2)),
                pltpu.SemaphoreType.DMA((2,)),
            ],
            input_output_aliases={3 + len(received): 0, 4 + len(received): 1},
            compiler_params=pltpu.CompilerParams(vmem_limit_bytes=48 << 20),
            cost_estimate=pl.CostEstimate(flops=25 * 4 * BS * BS * frames, bytes_accessed=8 << 20, transcendentals=0),
            name=("left_tiles", "right_tiles")[side],
        )(meta, edges, halo, *received, inst, lagg)
    return (inst, lagg)


def solution(mesh):
    in_specs = (P(AXES, None), P(AXES, None))
    out_specs = (P(AXES, None, None), P(AXES, None, None))
    return jax.shard_map(per_device, mesh=mesh, in_specs=in_specs, out_specs=out_specs, check_vma=False)
```

time: 105 us -> 105 us (level)
  waiting for transfers between devices: 42.2 us -> 44.6 us
  Pallas kernels: 28.4 us -> 26.5 us
  local copies, waits for them, and re-layouts: 1.39 us -> 0.17 us
    pallas_call x1, Pallas kernels: 16.8 us -> 14 us  [per_device(): pl.pallas_call(functools.partial(inner_kernel, blocks, (blocks,), tiles),...]
    all_to_all x1, waiting for transfers between devices: 1.22 us -> 3.56 us  [per_device(): lax.all_to_all(beside, AXES, split_axis=1, concat_axis=0, tiled=True)]
    unnamed x6 -> x4, local copies, waits for them, and re-layouts: 1.23 us -> 0.01 us
  transfers between devices with their start and end apart: 4 -> 4, of which waited for: 2 -> 2; matrix products, arithmetic and copies ran while one was open for 2% -> 2% of each run, Pallas kernels for 24% -> 20%
where the time goes in v4:
time: 105 us; the launch traced here: 104 us
  waiting for transfers between devices  44.6 us (42%)
  starting transfers between devices  29.8 us (28%)
  Pallas kernels  26.5 us (25%)
  other arithmetic  2.23 us (2%)
    all_to_all x1, waiting for transfers between devices, per_device(): lax.all_to_all(trajectory, AXES, split_axis=1, concat_axis=0, tiled=True)  41 us
    pallas_call x1, Pallas kernels, per_device(): pl.pallas_call(functools.partial(inner_kernel, blocks, (blocks,), tiles),...  14 us
    pallas_call x2, Pallas kernels, per_device(): pl.pallas_call(functools.partial(edge_kernel, blocks, side, bases[side],...  12.5 us
    all_to_all x1, starting transfers between devices, per_device(): lax.all_to_all(trajectory, AXES, split_axis=1, concat_axis=0, tiled=True)  11.9 us
    ppermute x1, starting transfers between devices, per_device(): far_r = lax.ppermute(to_left, AXES, [(i + 1, i) for i in range(count - 1)])  8.49 us
    all_to_all x1, starting transfers between devices, per_device(): lax.all_to_all(beside, AXES, split_axis=1, concat_axis=0, tiled=True)  6.18 us
    all_to_all x1, waiting for transfers between devices, per_device(): lax.all_to_all(beside, AXES, split_axis=1, concat_axis=0, tiled=True)  3.56 us
    ppermute x1, starting transfers between devices, per_device(): far_l = lax.ppermute(to_right, AXES, [(i, i + 1) for i in range(count - 1)])  3.22 us
  transfers between devices with their start and end apart: 4, of which 2 were waited for; matrix products, arithmetic and copies ran while one was open for 2% of the time, Pallas kernels for 20%

profile of v4, /device:TPU:1, one launch (start us, length us, event | category | flops | bytes accessed | tf_op | source)
XLA Modules:
  0.0 104.2 jit_solution(1670023076938735171)
XLA Ops:
  0.6 0.0 copy-start
  0.6 0.0 copy-start.1
  0.6 11.9 %all-to-all-start = ((bf16[8,128,1664]{2,0,1:T(8,128)(2,1)}), bf16[8,128,1664]{2,0,1:T(8,128)(2,1)}, u32[]{:S(2)}, u32[]{:S(2)}) async-start(bf16[8,128,1664]{2,0,1:T(8,128)(2,1)} %bitcast.93), calls=%async_computation | async-start | bytes 6815744 | tf_op jit(solution)/shard_map/all_to_all | solution.py:236
  12.6 0.0 copy-done.1
  12.7 0.2 convert_reduce_fusion
  12.8 0.1 select_reduce_fusion
  13.0 0.2 convert_reduce_fusion.1
  13.1 0.1 pad_add_fusion.meta_hbm
  13.2 0.0 copy-done
  13.2 0.2 fusion.25
  13.4 1.6 %fusion.2 = bf16[8,128,1024]{2,0,1:T(8,128)(2,1)} fusion(bf16[8,127,512]{2,0,1:T(8,128)(2,1)S(1)} %get-tuple-element.23, bf16[8,127,512]{2,0,1:T(8,128)(2,1)S(1)} %get-tuple-element.22), kind=kLoop, calls=%fused_computation.4 | loop fusion | flops 8388608 | bytes 4177920 | tf_op jit(solution)/shard_map/concatenate | solution.py:239
  15.0 41.0 %all-to-all-done = bf16[8,128,1664]{2,0,1:T(8,128)(2,1)} async-done(((bf16[8,128,1664]{2,0,1:T(8,128)(2,1)}), bf16[8,128,1664]{2,0,1:T(8,128)(2,1)}, u32[]{:S(2)}, u32[]{:S(2)}) %all-to-all-start) | async-done | bytes 3407904 | tf_op jit(solution)/shard_map/all_to_all | solution.py:236
  56.0 6.2 %all-to-all-start.1 = ((bf16[8,128,1024]{2,0,1:T(8,128)(2,1)}), bf16[8,128,1024]{2,0,1:T(8,128)(2,1)S(1)}, u32[]{:S(2)}, u32[]{:S(2)}) async-start(bf16[8,128,1024]{2,0,1:T(8,128)(2,1)} %fusion.2), calls=%async_computation.1 | async-start | bytes 4194304 | tf_op jit(solution)/shard_map/all_to_all | solution.py:249
  62.2 14.0 %inner_tiles.1 = (f32[96,128,128]{2,1,0:T(8,128)}, f32[96,128,128]{2,1,0:T(8,128)}, bf16[16,4,1024,128]{3,2,1,0:T(8,128)(2,1)}, bf16[384,256]{1,0:T(8,128)(2,1)S(1)}, bf16[384,256]{1,0:T(8,128)(2,1)S(1)}) custom-call(s32[128]{0:T(128)S(1)} %pad_add_fusion.meta_hbm, bf16[1024,1664]{1,0:T(8,128)(2,1)} %bitcast.2.own_ref), custom_call_target="tpu_custom_call" | custom-call | flops 7851737088 | bytes 20971520 | tf_op jit(solution)/shard_map/inner_tiles/pallas_call | solution.py:253
  76.2 3.2 %collective-permute-start = (bf16[384,256]{1,0:T(8,128)(2,1)S(1)}, bf16[384,256]{1,0:T(8,128)(2,1)S(1)}, u32[]{:S(2)}, u32[]{:S(2)}) collective-permute-start(bf16[384,256]{1,0:T(8,128)(2,1)S(1)} %get-tuple-element.16), channel_id=1, source_target_pairs={{0,1},{1,2},{2,3},{3,4},{4,5},{5,6},{6,7},{7,8},{8,9},{9,10},{10,1... | collective-permute-start | bytes 589832 | tf_op jit(solution)/shard_map/ppermute | solution.py:275
  79.5 8.5 %collective-permute-start.1 = (bf16[384,256]{1,0:T(8,128)(2,1)S(1)}, bf16[384,256]{1,0:T(8,128)(2,1)S(1)}, u32[]{:S(2)}, u32[]{:S(2)}) collective-permute-start(bf16[384,256]{1,0:T(8,128)(2,1)S(1)} %get-tuple-element.17), channel_id=1, source_target_pairs={{1,0},{2,1},{3,2},{4,3},{5,4},{6,5},{7,6},{8,7},{9,8},{10,9},{11,1... | collective-permute-start | bytes 589832 | tf_op jit(solution)/shard_map/ppermute | solution.py:274
  88.0 3.6 %all-to-all-done.1 = bf16[8,128,1024]{2,0,1:T(8,128)(2,1)S(1)} async-done(((bf16[8,128,1024]{2,0,1:T(8,128)(2,1)}), bf16[8,128,1024]{2,0,1:T(8,128)(2,1)S(1)}, u32[]{:S(2)}, u32[]{:S(2)}) %all-to-all-start.1) | async-done | bytes 2097184 | tf_op jit(solution)/shard_map/all_to_all | solution.py:249
  91.5 6.5 %left_tiles.1 = (f32[96,128,128]{2,1,0:T(8,128)}, f32[96,128,128]{2,1,0:T(8,128)}) custom-call(s32[128]{0:T(128)S(1)} %pad_add_fusion.meta_hbm, bf16[16,4,1024,128]{3,2,1,0:T(8,128)(2,1)} %get-tuple-element.14.edge_ref, bf16[1024,1024]{1,0:T(8,128)(2,1)S(1)} %bitcast.91, ...), custom_call_target="tpu_custom_call", output_to_operand_aliasing={{0}: (3, {}), {1}: (4, {})} | custom-call | flops 1677721600 | bytes 8388608 | tf_op jit(solution)/shard_map/left_tiles/pallas_call | solution.py:278
  98.0 0.0 collective-permute-done.refs_0_
  98.0 0.0 collective-permute-done.1.refs_1_
  98.0 6.0 %right_tiles.1 = (f32[96,128,128]{2,1,0:T(8,128)}, f32[96,128,128]{2,1,0:T(8,128)}) custom-call(s32[128]{0:T(128)S(1)} %pad_add_fusion.meta_hbm, bf16[16,4,1024,128]{3,2,1,0:T(8,128)(2,1)} %get-tuple-element.14.edge_ref, bf16[1024,1024]{1,0:T(8,128)(2,1)S(1)} %bitcast.92, ...), custom_call_target="tpu_custom_call", output_to_operand_aliasing={{0}: (5, {}), {1}: (6, {})} | custom-call | flops 1677721600 | bytes 8388608 | tf_op jit(solution)/shard_map/right_tiles/pallas_call | solution.py:278
  (5 shorter events, 0.1 us)
Async XLA Ops:
  0.6 12.6 %copy-start = (bf16[8,212992]{1,0:T(8,128)(2,1)S(1)}, bf16[8,212992]{1,0:T(8,128)(2,1)}, u32[]{:S(2)}) copy-start(bf16[8,212992]{1,0:T(8,128)(2,1)} %param.2) | copy-start | bytes 10223620
  0.6 11.9 %copy-start.1 = (s32[96,2]{0,1:T(2,128)S(1)}, s32[96,2]{0,1:T(2,128)}, u32[]{:S(2)}) copy-start(s32[96,2]{0,1:T(2,128)} %param.3) | copy-start | bytes 2308
  0.6 55.4 %all-to-all-start = ((bf16[8,128,1664]{2,0,1:T(8,128)(2,1)}), bf16[8,128,1664]{2,0,1:T(8,128)(2,1)}, u32[]{:S(2)}, u32[]{:S(2)}) async-start(bf16[8,128,1664]{2,0,1:T(8,128)(2,1)} %bitcast.93), calls=%async_computation | async-start | bytes 6815744 | tf_op jit(solution)/shard_map/all_to_all | solution.py:236
  56.0 35.5 %all-to-all-start.1 = ((bf16[8,128,1024]{2,0,1:T(8,128)(2,1)}), bf16[8,128,1024]{2,0,1:T(8,128)(2,1)S(1)}, u32[]{:S(2)}, u32[]{:S(2)}) async-start(bf16[8,128,1024]{2,0,1:T(8,128)(2,1)} %fusion.2), calls=%async_computation.1 | async-start | bytes 4194304 | tf_op jit(solution)/shard_map/all_to_all | solution.py:249
  76.2 21.8 %collective-permute-start = (bf16[384,256]{1,0:T(8,128)(2,1)S(1)}, bf16[384,256]{1,0:T(8,128)(2,1)S(1)}, u32[]{:S(2)}, u32[]{:S(2)}) collective-permute-start(bf16[384,256]{1,0:T(8,128)(2,1)S(1)} %get-tuple-element.16), channel_id=1, source_target_pairs={{0,1},{1,2},{2,3},{3,4},{4,5},{5,6},{6,7},{7,8},{8,9},{9,10},{10,1... | collective-permute-start | bytes 589832 | tf_op jit(solution)/shard_map/ppermute | solution.py:275
  79.5 18.6 %collective-permute-start.1 = (bf16[384,256]{1,0:T(8,128)(2,1)S(1)}, bf16[384,256]{1,0:T(8,128)(2,1)S(1)}, u32[]{:S(2)}, u32[]{:S(2)}) collective-permute-start(bf16[384,256]{1,0:T(8,128)(2,1)S(1)} %get-tuple-element.17), channel_id=1, source_target_pairs={{1,0},{2,1},{3,2},{4,3},{5,4},{6,5},{7,6},{8,7},{9,8},{10,9},{11,1... | collective-permute-start | bytes 589832 | tf_op jit(solution)/shard_map/ppermute | solution.py:274

commit v5 on v4

--- a/solution.py
+++ b/solution.py
@@ -187,8 +187,8 @@
         prod = jnp.dot(turned[block_rows(low, high), :], pair[slot], preferred_element_type=F32)
         for row in rows:
             keep(res, count + slot * ROWS + row, prod[block_rows(row - low, row - low + 1)], frames)
-        if slot in (HALO - 1, COLS - 1):
-            start_run(meta_ref, ends(group), ends(group + 1), *where)
+        if slot == COLS - 1 or (slot == HALO - 1 and side == 1):
+            start_run(meta_ref, ends(group), ends(blocks + 3 * side + (1 if slot < HALO else 2)), *where)
             group += 1
     wait_run(meta_ref, ends(blocks + 2 * side), ends(blocks + 2 + 3 * side), *where)
 

time: 105 us -> 104 us (level)
  transfers between devices with their start and end apart: 4 -> 4, of which waited for: 2 -> 2; matrix products, arithmetic and copies ran while one was open for 2% -> 2% of each run, Pallas kernels for 20% -> 19%
where the time goes in v5:
time: 104 us
  waiting for transfers between devices  44.4 us (43%)
  starting transfers between devices  29.8 us (29%)
  Pallas kernels  26.3 us (25%)
  other arithmetic  2.23 us (2%)
    all_to_all x1, waiting for transfers between devices, per_device(): lax.all_to_all(trajectory, AXES, split_axis=1, concat_axis=0, tiled=True)  41 us
    pallas_call x1, Pallas kernels, per_device(): pl.pallas_call(functools.partial(inner_kernel, blocks, (blocks,), tiles),...  14.2 us
    pallas_call x2, Pallas kernels, per_device(): pl.pallas_call(functools.partial(edge_kernel, blocks, side, bases[side],...  12.1 us
    all_to_all x1, starting transfers between devices, per_device(): lax.all_to_all(trajectory, AXES, split_axis=1, concat_axis=0, tiled=True)  11.9 us
    ppermute x1, starting transfers between devices, per_device(): far_r = lax.ppermute(to_left, AXES, [(i + 1, i) for i in range(count - 1)])  8.4 us
    all_to_all x1, starting transfers between devices, per_device(): lax.all_to_all(beside, AXES, split_axis=1, concat_axis=0, tiled=True)  6.18 us
    all_to_all x1, waiting for transfers between devices, per_device(): lax.all_to_all(beside, AXES, split_axis=1, concat_axis=0, tiled=True)  3.36 us
    ppermute x1, starting transfers between devices, per_device(): far_l = lax.ppermute(to_right, AXES, [(i, i + 1) for i in range(count - 1)])  3.31 us
  transfers between devices with their start and end apart: 4, of which 2 were waited for; matrix products, arithmetic and copies ran while one was open for 2% of the time, Pallas kernels for 19%

profile of v5, /device:TPU:1, one launch (start us, length us, event | category | flops | bytes accessed | tf_op | source)
XLA Modules:
  0.0 103.8 jit_solution(9933493222711029524)
XLA Ops:
  0.6 0.0 copy-start
  0.6 0.0 copy-start.1
  0.6 11.9 %all-to-all-start = ((bf16[8,128,1664]{2,0,1:T(8,128)(2,1)}), bf16[8,128,1664]{2,0,1:T(8,128)(2,1)}, u32[]{:S(2)}, u32[]{:S(2)}) async-start(bf16[8,128,1664]{2,0,1:T(8,128)(2,1)} %bitcast.93), calls=%async_computation | async-start | bytes 6815744 | tf_op jit(solution)/shard_map/all_to_all | solution.py:236
  12.6 0.0 copy-done.1
  12.7 0.2 convert_reduce_fusion
  12.8 0.1 select_reduce_fusion
  13.0 0.2 convert_reduce_fusion.1
  13.1 0.1 pad_add_fusion.meta_hbm
  13.2 0.0 copy-done
  13.2 0.2 fusion.25
  13.4 1.6 %fusion.2 = bf16[8,128,1024]{2,0,1:T(8,128)(2,1)} fusion(bf16[8,127,512]{2,0,1:T(8,128)(2,1)S(1)} %get-tuple-element.23, bf16[8,127,512]{2,0,1:T(8,128)(2,1)S(1)} %get-tuple-element.22), kind=kLoop, calls=%fused_computation.4 | loop fusion | flops 8388608 | bytes 4177920 | tf_op jit(solution)/shard_map/concatenate | solution.py:239
  15.0 41.0 %all-to-all-done = bf16[8,128,1664]{2,0,1:T(8,128)(2,1)} async-done(((bf16[8,128,1664]{2,0,1:T(8,128)(2,1)}), bf16[8,128,1664]{2,0,1:T(8,128)(2,1)}, u32[]{:S(2)}, u32[]{:S(2)}) %all-to-all-start) | async-done | bytes 3407904 | tf_op jit(solution)/shard_map/all_to_all | solution.py:236
  56.0 6.2 %all-to-all-start.1 = ((bf16[8,128,1024]{2,0,1:T(8,128)(2,1)}), bf16[8,128,1024]{2,0,1:T(8,128)(2,1)S(1)}, u32[]{:S(2)}, u32[]{:S(2)}) async-start(bf16[8,128,1024]{2,0,1:T(8,128)(2,1)} %fusion.2), calls=%async_computation.1 | async-start | bytes 4194304 | tf_op jit(solution)/shard_map/all_to_all | solution.py:249
  62.2 14.2 %inner_tiles.1 = (f32[96,128,128]{2,1,0:T(8,128)}, f32[96,128,128]{2,1,0:T(8,128)}, bf16[16,4,1024,128]{3,2,1,0:T(8,128)(2,1)}, bf16[384,256]{1,0:T(8,128)(2,1)S(1)}, bf16[384,256]{1,0:T(8,128)(2,1)S(1)}) custom-call(s32[128]{0:T(128)S(1)} %pad_add_fusion.meta_hbm, bf16[1024,1664]{1,0:T(8,128)(2,1)} %bitcast.2.own_ref), custom_call_target="tpu_custom_call" | custom-call | flops 7851737088 | bytes 20971520 | tf_op jit(solution)/shard_map/inner_tiles/pallas_call | solution.py:253
  76.4 3.3 %collective-permute-start = (bf16[384,256]{1,0:T(8,128)(2,1)S(1)}, bf16[384,256]{1,0:T(8,128)(2,1)S(1)}, u32[]{:S(2)}, u32[]{:S(2)}) collective-permute-start(bf16[384,256]{1,0:T(8,128)(2,1)S(1)} %get-tuple-element.16), channel_id=1, source_target_pairs={{0,1},{1,2},{2,3},{3,4},{4,5},{5,6},{6,7},{7,8},{8,9},{9,10},{10,1... | collective-permute-start | bytes 589832 | tf_op jit(solution)/shard_map/ppermute | solution.py:275
  79.7 8.4 %collective-permute-start.1 = (bf16[384,256]{1,0:T(8,128)(2,1)S(1)}, bf16[384,256]{1,0:T(8,128)(2,1)S(1)}, u32[]{:S(2)}, u32[]{:S(2)}) collective-permute-start(bf16[384,256]{1,0:T(8,128)(2,1)S(1)} %get-tuple-element.17), channel_id=1, source_target_pairs={{1,0},{2,1},{3,2},{4,3},{5,4},{6,5},{7,6},{8,7},{9,8},{10,9},{11,1... | collective-permute-start | bytes 589832 | tf_op jit(solution)/shard_map/ppermute | solution.py:274
  88.1 3.4 %all-to-all-done.1 = bf16[8,128,1024]{2,0,1:T(8,128)(2,1)S(1)} async-done(((bf16[8,128,1024]{2,0,1:T(8,128)(2,1)}), bf16[8,128,1024]{2,0,1:T(8,128)(2,1)S(1)}, u32[]{:S(2)}, u32[]{:S(2)}) %all-to-all-start.1) | async-done | bytes 2097184 | tf_op jit(solution)/shard_map/all_to_all | solution.py:249
  91.5 6.0 %left_tiles.1 = (f32[96,128,128]{2,1,0:T(8,128)}, f32[96,128,128]{2,1,0:T(8,128)}) custom-call(s32[128]{0:T(128)S(1)} %pad_add_fusion.meta_hbm, bf16[16,4,1024,128]{3,2,1,0:T(8,128)(2,1)} %get-tuple-element.14.edge_ref, bf16[1024,1024]{1,0:T(8,128)(2,1)S(1)} %bitcast.91, ...), custom_call_target="tpu_custom_call", output_to_operand_aliasing={{0}: (3, {}), {1}: (4, {})} | custom-call | flops 1677721600 | bytes 8388608 | tf_op jit(solution)/shard_map/left_tiles/pallas_call | solution.py:278
  97.6 0.0 collective-permute-done.refs_0_
  97.6 0.0 collective-permute-done.1.refs_1_
  97.6 6.1 %right_tiles.1 = (f32[96,128,128]{2,1,0:T(8,128)}, f32[96,128,128]{2,1,0:T(8,128)}) custom-call(s32[128]{0:T(128)S(1)} %pad_add_fusion.meta_hbm, bf16[16,4,1024,128]{3,2,1,0:T(8,128)(2,1)} %get-tuple-element.14.edge_ref, bf16[1024,1024]{1,0:T(8,128)(2,1)S(1)} %bitcast.92, ...), custom_call_target="tpu_custom_call", output_to_operand_aliasing={{0}: (5, {}), {1}: (6, {})} | custom-call | flops 1677721600 | bytes 8388608 | tf_op jit(solution)/shard_map/right_tiles/pallas_call | solution.py:278
  (5 shorter events, 0.1 us)
Async XLA Ops:
  0.6 12.6 %copy-start = (bf16[8,212992]{1,0:T(8,128)(2,1)S(1)}, bf16[8,212992]{1,0:T(8,128)(2,1)}, u32[]{:S(2)}) copy-start(bf16[8,212992]{1,0:T(8,128)(2,1)} %param.2) | copy-start | bytes 10223620
  0.6 11.9 %copy-start.1 = (s32[96,2]{0,1:T(2,128)S(1)}, s32[96,2]{0,1:T(2,128)}, u32[]{:S(2)}) copy-start(s32[96,2]{0,1:T(2,128)} %param.3) | copy-start | bytes 2308
  0.6 55.4 %all-to-all-start = ((bf16[8,128,1664]{2,0,1:T(8,128)(2,1)}), bf16[8,128,1664]{2,0,1:T(8,128)(2,1)}, u32[]{:S(2)}, u32[]{:S(2)}) async-start(bf16[8,128,1664]{2,0,1:T(8,128)(2,1)} %bitcast.93), calls=%async_computation | async-start | bytes 6815744 | tf_op jit(solution)/shard_map/all_to_all | solution.py:236
  56.0 35.5 %all-to-all-start.1 = ((bf16[8,128,1024]{2,0,1:T(8,128)(2,1)}), bf16[8,128,1024]{2,0,1:T(8,128)(2,1)S(1)}, u32[]{:S(2)}, u32[]{:S(2)}) async-start(bf16[8,128,1024]{2,0,1:T(8,128)(2,1)} %fusion.2), calls=%async_computation.1 | async-start | bytes 4194304 | tf_op jit(solution)/shard_map/all_to_all | solution.py:249
  76.4 21.1 %collective-permute-start = (bf16[384,256]{1,0:T(8,128)(2,1)S(1)}, bf16[384,256]{1,0:T(8,128)(2,1)S(1)}, u32[]{:S(2)}, u32[]{:S(2)}) collective-permute-start(bf16[384,256]{1,0:T(8,128)(2,1)S(1)} %get-tuple-element.16), channel_id=1, source_target_pairs={{0,1},{1,2},{2,3},{3,4},{4,5},{5,6},{6,7},{7,8},{8,9},{9,10},{10,1... | collective-permute-start | bytes 589832 | tf_op jit(solution)/shard_map/ppermute | solution.py:275
  79.7 17.8 %collective-permute-start.1 = (bf16[384,256]{1,0:T(8,128)(2,1)S(1)}, bf16[384,256]{1,0:T(8,128)(2,1)S(1)}, u32[]{:S(2)}, u32[]{:S(2)}) collective-permute-start(bf16[384,256]{1,0:T(8,128)(2,1)S(1)} %get-tuple-element.17), channel_id=1, source_target_pairs={{1,0},{2,1},{3,2},{4,3},{5,4},{6,5},{7,6},{8,7},{9,8},{10,9},{11,1... | collective-permute-start | bytes 589832 | tf_op jit(solution)/shard_map/ppermute | solution.py:274
